TPU v7x, 512 devices: a whole 4x4x16 slice. The times are simulated.
512 devices in a mesh: row: 8 (over z_lo), col: 16 (over z_hi, x, core), dp: 4 (over y).
Axes of the slice: x: 4, y: 4, z: 16 (z_hi: 2, z_lo: 8; z = z_hi * 8 + z_lo), core: 2. Of those that a mesh axis runs over, the one named last changes fastest.
Arguments:
- tokens: bfloat16 [640, 6144], P(('col', 'dp'), 'row'), may hold values from -6 to 6
- in_weight: bfloat16 [6144, 24576], P('row', ('col', 'dp')), may hold values from -0.078125 to 0.078125
- out_weight: bfloat16 [24576, 6144], P(('col', 'dp'), 'row'), may hold values from -0.0390625 to 0.0390625
- cotangent: bfloat16 [640, 6144], P(('col', 'dp'), 'row'), may hold values from -1.5 to 1.5
Outputs:
- mixed: bfloat16 [640, 6144], P(('col', 'dp'), 'row')
- token_grad: bfloat16 [640, 6144], P(('col', 'dp'), 'row')
- in_grad: float32 [6144, 24576], P('row', ('col', 'dp'))
- out_grad: float32 [24576, 6144], P(('col', 'dp'), 'row')
All inputs are finite; a program needn't handle non-finite values.
Results may differ from a plain program's by a relative error of at most 0.02.
Values may be sent and summed in bfloat16 or wider, within the bound.
No kernel may reach another device: no remote copies, remote signals or barrier semaphores. Data moves between devices by JAX's collectives and lax.ppermute only.
A program may use at most 64 MiB of HBM per device.

v0:
```python
import jax
import jax.numpy as jnp
from jax import lax
from jax.sharding import PartitionSpec as P


def gelu_value(h):
    inner = 0.7978845608 * (h + 0.044715 * h * h * h)
    return 0.5 * h * (1.0 + jnp.tanh(inner))


def gelu_slope(h):
    inner = 0.7978845608 * (h + 0.044715 * h * h * h)
    t = jnp.tanh(inner)
    return 0.5 * (1.0 + t) + 0.5 * h * (1.0 - t * t) * 0.7978845608 * (1.0 + 3.0 * 0.044715 * h * h)


def gather_panel(local):
    return lax.all_gather(local, ("col", "dp"), axis=0, tiled=True)


def sum_rows(term_fn, kept):
    return lax.psum_scatter(
        term_fn(jnp.int32(0), kept * lax.axis_size(("col", "dp"))),
        ("col", "dp"),
        scatter_dimension=0,
        tiled=True,
    )


def body(tokens, in_weight, out_weight, cotangent):
    kept = tokens.shape[0]
    panel = gather_panel(tokens)
    partial_value = jnp.dot(panel, in_weight, preferred_element_type=jnp.float32)
    hidden = lax.psum(partial_value.astype(jnp.bfloat16), "row").astype(jnp.float32)
    acts = gelu_value(hidden).astype(jnp.bfloat16)

    def out_terms(start, count):
        return jnp.dot(acts, out_weight, preferred_element_type=jnp.float32)

    mixed = (tokens.astype(jnp.float32) + sum_rows(out_terms, kept)).astype(jnp.bfloat16)
    cot_panel = gather_panel(cotangent)
    back_part = lax.dot_general(
        cot_panel, out_weight, (((1,), (1,)), ((), ())), preferred_element_type=jnp.float32
    )
    act_grad = lax.psum(back_part.astype(jnp.bfloat16), "row").astype(jnp.float32)
    hid_grad = (act_grad * gelu_slope(hidden)).astype(jnp.bfloat16)

    def in_terms(start, count):
        return lax.dot_general(
            hid_grad, in_weight, (((1,), (1,)), ((), ())), preferred_element_type=jnp.float32
        )

    token_grad = (cotangent.astype(jnp.float32) + sum_rows(in_terms, kept)).astype(jnp.bfloat16)
    in_grad = lax.dot_general(
        panel, hid_grad, (((0,), (0,)), ((), ())), preferred_element_type=jnp.float32
    )
    out_grad = lax.dot_general(
        acts, cot_panel, (((0,), (0,)), ((), ())), preferred_element_type=jnp.float32
    )
    return (mixed, token_grad, in_grad, out_grad)


def solution(mesh):
    return jax.shard_map(
        body,
        mesh=mesh,
        in_specs=(
            P(("col", "dp"), "row"),
            P("row", ("col", "dp")),
            P(("col", "dp"), "row"),
            P(("col", "dp"), "row"),
        ),
        out_specs=(
            P(("col", "dp"), "row"),
            P(("col", "dp"), "row"),
            P("row", ("col", "dp")),
            P(("col", "dp"), "row"),
        ),
        check_vma=False,
    )
```

profile of v0, /device:TPU:1, one launch (start us, length us, event | category | flops | bytes accessed | tf_op | source)
XLA Modules:
  0.0 1806.2 jit_solution(2002532794016791247)
XLA Ops:
  7.2 0.0 copy-start
  7.2 0.0 all-reduce.9.cloned.1.call-start
  7.2 0.0 copy-start.2
  7.2 279.6 %all-gather.1 = bf16[64,10,768]{2,1,0:T(8,128)(2,1)S(1)} all-gather(bf16[1,10,768]{2,1,0:T(8,128)(2,1)} %bitcast.14), channel_id=1, replica_groups=mesh['row'=8,'col'=16,'dp'=4] {'col','dp'}, dimensions={0}, use_global_device_ids=true | all-gather | bytes 998400 | tf_op jit(solution)/shard_map/all_gather | solution.py:19
  286.8 0.4 reshape.11
  287.2 0.0 copy-done.2
  287.2 283.7 %all-gather = bf16[64,10,768]{2,1,0:T(8,128)(2,1)S(1)} all-gather(bf16[1,10,768]{2,1,0:T(8,128)(2,1)S(1)} %bitcast.13), channel_id=1, replica_groups=mesh['row'=8,'col'=16,'dp'=4] {'col','dp'}, dimensions={0}, use_global_device_ids=true | all-gather | bytes 998400 | tf_op jit(solution)/shard_map/all_gather | solution.py:19
  570.9 1.1 reshape.9
  572.1 0.0 copy-done
  572.1 0.0 copy-start.1
  572.1 0.0 copy-start.4
  572.1 1.5 convolution_convert_fusion
  573.6 0.0 copy-done.1
  573.6 0.0 copy-done.4
  573.6 1.5 convolution_convert_fusion.1
  575.0 0.0 all-reduce.9.cloned.1.call-update
  575.0 0.0 all-reduce.7.cloned.1.call-start
  575.1 136.8 %all-reduce.9.cloned.1.call-done = (bf16[640,384]{1,0:T(8,128)(2,1)}, bf16[640,384]{1,0:T(8,128)(2,1)}) async-done(((bf16[640,384]{1,0:T(8,128)(2,1)}, bf16[640,384]{1,0:T(8,128)(2,1)}), (bf16[640,384]{1,0:T(8,128)(2,1)}, bf16[640,384]{1,0:T(8,128)(2,1)})) %all-reduce.9.cloned.1.call-update) | async-done | bytes 983056 | tf_op jit(solution)/shard_map/psum | solution.py:35
  711.9 0.0 copy-start.5
  711.9 0.0 copy-start.6
  711.9 3.2 fusion.15
  715.1 0.0 copy-done.5
  715.1 0.0 copy-done.6
  715.1 2.5 fusion.18
  717.6 0.0 all-reduce.7.cloned.1.call-update
  717.6 1.3 dynamic-slice
  719.5 2.4 convolution_bitcast_fusion
  722.0 1.4 copy.10
  723.3 0.0 copy-start.3
  723.3 1.8 fusion.13
  725.2 1072.6 %all-reduce.7.cloned.1.call-done = (f32[640,768]{1,0:T(8,128)}, f32[640,768]{1,0:T(8,128)}) async-done(((f32[640,768]{1,0:T(8,128)}, f32[640,768]{1,0:T(8,128)}), (f32[640,768]{1,0:T(8,128)}, f32[640,768]{1,0:T(8,128)})) %all-reduce.7.cloned.1.call-update) | async-done | bytes 3932176
  1797.8 0.0 copy-done.3
  1797.8 1.6 fusion.11
Async XLA Ops:
  7.2 564.9 %copy-start = (bf16[384,768]{1,0:T(8,128)(2,1)S(1)}, bf16[384,768]{1,0:T(8,128)(2,1)}, u32[]{:S(2)}) copy-start(bf16[384,768]{1,0:T(8,128)(2,1)} %param.6) | copy-start | bytes 1769476
  7.2 704.7 %all-reduce.9.cloned.1.call-start = ((), (), s32[]{:S(2)}) async-start(), calls=%async_computation.1 | async-start | bytes 1966080 | tf_op jit(solution)/shard_map/psum | solution.py:35
  7.2 280.0 %copy-start.2 = (bf16[10,768]{1,0:T(8,128)(2,1)S(1)}, bf16[10,768]{1,0:T(8,128)(2,1)}, u32[]{:S(2)}) copy-start(bf16[10,768]{1,0:T(8,128)(2,1)} %param.4) | copy-start | bytes 46084
  572.1 1.5 copy-start.1
  572.1 1.5 copy-start.4
  575.0 1222.7 %all-reduce.7.cloned.1.call-start = ((), (), s32[]{:S(2)}) async-start(), calls=%async_computation | async-start | bytes 7864320
  711.9 3.2 copy-start.5
  711.9 3.2 copy-start.6
  723.3 1074.4 %copy-start.3 = (bf16[10,768]{1,0:T(8,128)(2,1)S(1)}, bf16[10,768]{1,0:T(8,128)(2,1)}, u32[]{:S(2)}) copy-start(bf16[10,768]{1,0:T(8,128)(2,1)} %param.7) | copy-start | bytes 46084
Sparse Core Ops, SparseCore 0:
  575.2 136.6 all-reduce.8
  717.7 1080.0 all-reduce.6
where the time goes:
time: 1810 us
  waiting for transfers between devices  1210 us (67%)
  blocking collectives  563 us (31%)
    unnamed x3, waiting for transfers between devices  1070 us
    all_gather x2, blocking collectives, gather_panel(): return lax.all_gather(local, ('col', 'dp'), axis=0, tiled=True)  563 us
    psum x1, waiting for transfers between devices, body(): lax.psum(partial_value.astype(jnp.bfloat16), 'row').astype(jnp.float32)  137 us
  transfers between devices with their start and end apart: 2, of which 2 were waited for; matrix products, arithmetic and copies ran while one was open for 0% of the time, Pallas kernels for 0%

commit v1 on v0

v1 whole, which is shorter than its diff:
```python
import jax
import jax.numpy as jnp
from jax import lax
from jax.experimental import pallas as pl
from jax.experimental.pallas import tpu as pltpu
from jax.sharding import Mesh
from jax.sharding import PartitionSpec as P

ROW = ("za", "zb", "zc")
CD = ("zhi", "x", "core", "y")
XY = ("x", "y")
SWAP = [(0, 1), (1, 0)]
F32 = jnp.float32
BF16 = jnp.bfloat16
NT = (((1,), (1,)), ((), ()))
TN = (((0,), (0,)), ((), ()))


def gelu_value(h):
    inner = 0.7978845608 * (h + 0.044715 * h * h * h)
    return 0.5 * h * (1.0 + jnp.tanh(inner))


def gelu_slope(h):
    inner = 0.7978845608 * (h + 0.044715 * h * h * h)
    t = jnp.tanh(inner)
    return 0.5 * (1.0 + t) + 0.5 * h * (1.0 - t * t) * 0.7978845608 * (1.0 + 3.0 * 0.044715 * h * h)


def first_kernel(place, x, a, b, send, keep, ordered):
    r, role = place[0], place[1]
    rows = x.shape[1]
    half = 4 * rows
    width = a.shape[2]
    for j in range(8):
        ordered[rows * j : rows * (j + 1), :] = x[lax.bitwise_xor(r, j)]

    @pl.when(role == 0)
    def _():
        for c in range(2):
            cols = slice(width * c, width * (c + 1))
            send[:, cols] = jnp.dot(ordered[half:, :], a[c], preferred_element_type=F32).astype(BF16)
            keep[:, cols] = jnp.dot(ordered[:half, :], a[c], preferred_element_type=F32)

    @pl.when(role == 1)
    def _():
        for c in range(2):
            cols = slice(width * c, width * (c + 1))
            part = b[cols, :]
            send[:, cols] = lax.dot_general(ordered[half:, :], part, NT, preferred_element_type=F32).astype(BF16)
            keep[:, cols] = lax.dot_general(ordered[:half, :], part, NT, preferred_element_type=F32)


def second_kernel(place, low, high, a, b, out):
    r, role = place[0], place[1]
    rows = out.shape[1]
    width = a.shape[2]

    def put(first, product):
        for j in range(4):
            out[lax.bitwise_xor(r, first + j)] = product[rows * j : rows * (j + 1), :].astype(BF16)

    for first, g in ((0, low), (4, high)):

        @pl.when(role == 0)
        def _():
            put(first, jnp.dot(g[...], b[...], preferred_element_type=F32))

        @pl.when(role == 1)
        def _():
            put(
                first,
                lax.dot_general(g[:, :width], a[0], NT, preferred_element_type=F32)
                + lax.dot_general(g[:, width:], a[1], NT, preferred_element_type=F32),
            )


def call(kernel, outs, place, *arrays):
    whole = pl.BlockSpec(memory_space=pltpu.VMEM)
    return pl.pallas_call(
        kernel,
        out_shape=outs,
        in_specs=[pl.BlockSpec(memory_space=pltpu.SMEM)] + [whole] * len(arrays),
        out_specs=jax.tree.map(lambda _: whole, outs),
        compiler_params=pltpu.CompilerParams(vmem_limit_bytes=40 * 1024 * 1024),
        cost_estimate=pl.CostEstimate(flops=2 * 640 * 768 * 768, bytes_accessed=6_000_000, transcendentals=0),
    )(place, *arrays)


def swap(x, axis):
    return lax.ppermute(x, axis, SWAP)


def body(tokens, in_weight, out_weight, cotangent):
    kept, feats = tokens.shape
    width = in_weight.shape[1]
    core = lax.axis_index("core")
    r = 4 * lax.axis_index("zc") + 2 * lax.axis_index("zb") + lax.axis_index("za")
    place = jnp.stack([r, core]).astype(jnp.int32)
    is_first = core == 0

    both = lax.all_gather(jnp.concatenate([tokens, cotangent], axis=1), "core", tiled=True)
    mine = jnp.where(is_first, both[:, :feats], both[:, feats:])
    pair = jnp.concatenate([mine, swap(mine, "zhi")], axis=0)
    a = lax.all_gather(in_weight, "core")
    b = lax.all_gather(out_weight, "core", tiled=True)
    panel = lax.all_to_all(jnp.broadcast_to(pair[None], (16,) + pair.shape), XY, 0, 0, tiled=True)
    panel = panel.reshape(8, 8 * kept, feats)
    rows = 8 * kept

    send, keep, ordered = call(
        first_kernel,
        (
            jax.ShapeDtypeStruct((4 * rows, 2 * width), BF16),
            jax.ShapeDtypeStruct((4 * rows, 2 * width), F32),
            jax.ShapeDtypeStruct((8 * rows, feats), BF16),
        ),
        place,
        panel,
        a,
        b,
    )
    panels = lax.all_gather(ordered, "core")

    for axis, count in (("zc", 2), ("zb", 1), ("za", 0)):
        came = swap(send, axis)
        if count:
            cut = count * rows
            send = (keep[cut:] + came[cut:].astype(F32)).astype(BF16)
            keep = keep[:cut] + came[:cut].astype(F32)
        else:
            keep = keep + came.astype(F32)

    other = swap(keep, "core")
    block = jnp.where(is_first, gelu_value(keep), keep * gelu_slope(other)).astype(BF16)

    block = jnp.concatenate([block, swap(block, "za")], axis=0)
    block = jnp.concatenate([block, swap(block, "zb")], axis=0)
    high = swap(block, "zc")

    part = call(second_kernel, jax.ShapeDtypeStruct((8, rows, feats), BF16), place, block, high, a, b)
    grads = lax.all_gather(jnp.concatenate([block, high], axis=0), "core")

    parts = lax.all_to_all(part.reshape(16, 4 * kept, feats), XY, 0, 0, tiled=True)
    sums = jnp.sum(parts.astype(F32), axis=0)
    sums = sums[: 2 * kept] + swap(sums[2 * kept :].astype(BF16), "zhi").astype(F32)
    got = swap(jnp.where(is_first, sums[kept:], sums[:kept]), "core")
    mixed = (tokens.astype(F32) + jnp.where(is_first, sums[:kept], got)).astype(BF16)
    token_grad = (cotangent.astype(F32) + jnp.where(is_first, got, sums[kept:])).astype(BF16)

    acts = lax.dynamic_slice_in_dim(grads[0], core * width, width, axis=1)
    hid_grad = lax.dynamic_slice_in_dim(grads[1], core * width, width, axis=1)
    in_grad = lax.dot_general(panels[0], hid_grad, TN, preferred_element_type=F32)
    out_grad = lax.dot_general(acts, panels[1], TN, preferred_element_type=F32)
    return (mixed, token_grad, in_grad, out_grad)


def solution(mesh):
    fine = Mesh(mesh.devices.reshape(2, 2, 2, 2, 4, 2, 4), ROW + CD)
    return jax.shard_map(
        body,
        mesh=fine,
        in_specs=(P(CD, ROW), P(ROW, CD), P(CD, ROW), P(CD, ROW)),
        out_specs=(P(CD, ROW), P(CD, ROW), P(ROW, CD), P(CD, ROW)),
        check_vma=False,
    )
```

time: 1810 us -> 220 us (0.12)
  waiting for transfers between devices: 1210 us -> 122 us
  blocking collectives: 563 us -> 8.4 us
  starting transfers between devices: 0.08 us -> 56.8 us
    unnamed x3 -> x4, waiting for transfers between devices: 1070 us -> 1.92 us
    all_gather x2 -> x1, blocking collectives: 563 us -> 8.4 us  [body(): lax.all_gather(jnp.concatenate([tokens, cotangent], axis=1), 'core', tile...]
    psum x1 -> x0, waiting for transfers between devices: 137 us -> none  [body(): lax.psum(partial_value.astype(jnp.bfloat16), 'row').astype(jnp.float32)]
    ppermute x0 -> x10, waiting for transfers between devices: none -> 83.3 us  [swap(): return lax.ppermute(x, axis, SWAP)]
    ppermute x0 -> x10, starting transfers between devices: none -> 45.7 us  [swap(): return lax.ppermute(x, axis, SWAP)]
    all_to_all x0 -> x2, waiting for transfers between devices: none -> 28.3 us  [the longest x1 14.3 us: body(): lax.all_to_all(jnp.broadcast_to(pair[None], (16,) + pair.shape), XY, 0, 0...]
  transfers between devices with their start and end apart: 2 -> 16, of which waited for: 2 -> 13; matrix products, arithmetic and copies ran while one was open for 0% -> 2% of each run, Pallas kernels for 0% -> 1%
where the time goes in v1:
time: 220 us
  waiting for transfers between devices  122 us (55%)
  starting transfers between devices  56.8 us (26%)
  between operations  14 us (6%)
  blocking collectives  8.4 us (4%)
  Pallas kernels  5.66 us (3%)
  local copies, waits for them, and re-layouts  5.23 us (2%)
  matrix products  4.85 us (2%)
  other arithmetic  3.18 us (1%)
    ppermute x10, waiting for transfers between devices, swap(): return lax.ppermute(x, axis, SWAP)  83.3 us
    ppermute x10, starting transfers between devices, swap(): return lax.ppermute(x, axis, SWAP)  45.7 us
    all_to_all x1, waiting for transfers between devices, body(): lax.all_to_all(jnp.broadcast_to(pair[None], (16,) + pair.shape), XY, 0, 0...  14.3 us
    all_to_all x1, waiting for transfers between devices, body(): lax.all_to_all(part.reshape(16, 4 * kept, feats), XY, 0, 0, tiled=True)  14 us
    all_gather x1, blocking collectives, body(): lax.all_gather(jnp.concatenate([tokens, cotangent], axis=1), 'core', tile...  8.4 us
    all_gather x1, waiting for transfers between devices, body(): b = lax.all_gather(out_weight, 'core', tiled=True)  8.11 us
    all_to_all x1, starting transfers between devices, body(): lax.all_to_all(part.reshape(16, 4 * kept, feats), XY, 0, 0, tiled=True)  6.02 us
    pallas_call x2, Pallas kernels, call(): pl.pallas_call(kernel, out_shape=outs, in_specs=[pl.BlockSpec(memory_spac...  5.66 us
  transfers between devices with their start and end apart: 16, of which 13 were waited for; matrix products, arithmetic and copies ran while one was open for 2% of the time, Pallas kernels for 1%

profile of v1, /device:TPU:1, one launch (start us, length us, event | category | flops | bytes accessed | tf_op | source)
XLA Modules:
  0.0 219.7 jit_solution(639978798855934031)
XLA Ops:
  7.2 0.0 all-gather.11.cloned.1.call-start
  7.2 0.7 all-gather.11.cloned.1.call-update
  7.9 0.0 all-gather.9.cloned.1.call-start
  7.9 0.7 all-gather.9.cloned.1.call-update
  8.7 0.8 maximum_bitcast_fusion
  9.4 8.4 %all-gather.3 = bf16[2,10,1536]{2,1,0:T(8,128)(2,1)S(1)} all-gather(bf16[1,10,1536]{2,1,0:T(8,128)(2,1)S(1)} %maximum_bitcast_fusion), channel_id=1, replica_groups=mesh['za'=2,'zb'=2,'zc'=2,'zhi'=2,'x'=4,'core'=2,'y'=4] {'core'}, dimensions={0}, use_global_device_ids=true | all-gather | bytes 92160 | tf_op jit(solution)/shard_map/all_gather | solution.py:102
  17.9 10.1 %collective-permute-start = (bf16[20,768]{1,0:T(8,128)(2,1)S(1)}, bf16[20,768]{1,0:T(8,128)(2,1)S(1)}, u32[]{:S(2)}, u32[]{:S(2)}) collective-permute-start(bf16[20,768]{1,0:T(8,128)(2,1)S(1)} %slice_select_fusion.1), channel_id=1, source_target_pairs={{0,32},{32,0},{1,33},{33,1},{2,34},{34,2},{3,35},{35,3},{4,36},{36... | collective-permute-start | bytes 92168 | tf_op jit(solution)/shard_map/ppermute | solution.py:91
  27.9 3.3 %collective-permute-done = bf16[20,768]{1,0:T(8,128)(2,1)S(1)} collective-permute-done((bf16[20,768]{1,0:T(8,128)(2,1)S(1)}, bf16[20,768]{1,0:T(8,128)(2,1)S(1)}, u32[]{:S(2)}, u32[]{:S(2)}) %collective-permute-start) | collective-permute-done | bytes 30752 | tf_op jit(solution)/shard_map/ppermute | solution.py:91
  31.3 1.0 broadcast_in_dim.2
  32.3 4.9 %all-to-all-start = ((bf16[16,40,768]{2,1,0:T(8,128)(2,1)}), bf16[16,40,768]{2,1,0:T(8,128)(2,1)S(1)}, u32[]{:S(2)}, u32[]{:S(2)}) async-start(bf16[16,40,768]{2,1,0:T(8,128)(2,1)} %broadcast_in_dim.2), calls=%async_computation | async-start | bytes 1966080 | tf_op jit(solution)/shard_map/all_to_all | solution.py:107
  37.2 0.0 all-gather.15.cloned.1.call-start
  37.3 0.1 pad_add_fusion.place
  37.3 14.3 %all-to-all-done = bf16[16,40,768]{2,1,0:T(8,128)(2,1)S(1)} async-done(((bf16[16,40,768]{2,1,0:T(8,128)(2,1)}), bf16[16,40,768]{2,1,0:T(8,128)(2,1)S(1)}, u32[]{:S(2)}, u32[]{:S(2)}) %all-to-all-start) | async-done | bytes 983072 | tf_op jit(solution)/shard_map/all_to_all | solution.py:107
  51.6 8.1 %all-gather.9.cloned.1.call-done.b = bf16[768,768]{1,0:T(8,128)(2,1)} async-done(((bf16[384,768]{1,0:T(8,128)(2,1)}), bf16[768,768]{1,0:T(8,128)(2,1)}) %all-gather.9.cloned.1.call-update) | async-done | bytes 1179664 | tf_op jit(solution)/shard_map/all_gather | solution.py:106
  59.7 1.3 copy-done
  61.0 1.3 copy-done.2
  62.3 2.7 %shard_map.75 = (bf16[320,768]{1,0:T(8,128)(2,1)S(1)}, f32[320,768]{1,0:T(8,128)S(1)}, bf16[640,768]{1,0:T(8,128)(2,1)}) custom-call(s32[2]{0:T(128)S(1)} %pad_add_fusion.place, bf16[8,80,768]{2,1,0:T(8,128)(2,1)S(1)} %bitcast.9, bf16[2,768,384]{2,1,0:T(8,128)(2,1)S(1)} %bitcast.7, bf16[768,768]{1,0:T(8,128)(2,1)S(1)} %copy-done.2), custom_call_target="tpu_custom_call" | custom-call | flops 754974720 | bytes 6000000 | tf_op jit(solution)/shard_map/pallas_call | solution.py:80
  65.0 2.2 collective-permute-start.1
  67.2 12.3 %collective-permute-done.1 = bf16[320,768]{1,0:T(8,128)(2,1)S(1)} collective-permute-done((bf16[320,768]{1,0:T(8,128)(2,1)S(1)}, bf16[320,768]{1,0:T(8,128)(2,1)S(1)}, u32[]{:S(2)}, u32[]{:S(2)}) %collective-permute-start.1) | collective-permute-done | bytes 491552 | tf_op jit(solution)/shard_map/ppermute | solution.py:91
  79.5 0.1 add_convert_fusion
  79.6 3.2 %collective-permute-start.2 = (bf16[160,768]{1,0:T(8,128)(2,1)S(1)}, bf16[160,768]{1,0:T(8,128)(2,1)S(1)}, u32[]{:S(2)}, u32[]{:S(2)}) collective-permute-start(bf16[160,768]{1,0:T(8,128)(2,1)S(1)} %get-tuple-element.12), channel_id=1, source_target_pairs={{0,128},{128,0},{1,129},{129,1},{2,130},{130,2},{3,131},{131,3},{4... | collective-permute-start | bytes 737288 | tf_op jit(solution)/shard_map/ppermute | solution.py:91
  82.8 12.8 %collective-permute-done.2 = bf16[160,768]{1,0:T(8,128)(2,1)S(1)} collective-permute-done((bf16[160,768]{1,0:T(8,128)(2,1)S(1)}, bf16[160,768]{1,0:T(8,128)(2,1)S(1)}, u32[]{:S(2)}, u32[]{:S(2)}) %collective-permute-start.2) | collective-permute-done | bytes 245792 | tf_op jit(solution)/shard_map/ppermute | solution.py:91
  95.6 5.3 %collective-permute-start.3 = (bf16[80,768]{1,0:T(8,128)(2,1)S(1)}, bf16[80,768]{1,0:T(8,128)(2,1)S(1)}, u32[]{:S(2)}, u32[]{:S(2)}) collective-permute-start(bf16[80,768]{1,0:T(8,128)(2,1)S(1)} %fusion.18), channel_id=1, source_target_pairs={{0,256},{256,0},{1,257},{257,1},{2,258},{258,2},{3,259},{259,3},{4... | collective-permute-start | bytes 368648 | tf_op jit(solution)/shard_map/ppermute | solution.py:91
  100.9 12.6 %collective-permute-done.3 = bf16[80,768]{1,0:T(8,128)(2,1)S(1)} collective-permute-done((bf16[80,768]{1,0:T(8,128)(2,1)S(1)}, bf16[80,768]{1,0:T(8,128)(2,1)S(1)}, u32[]{:S(2)}, u32[]{:S(2)}) %collective-permute-start.3) | collective-permute-done | bytes 122912 | tf_op jit(solution)/shard_map/ppermute | solution.py:91
  113.5 2.4 %collective-permute-start.4 = (f32[80,768]{1,0:T(8,128)S(1)}, f32[80,768]{1,0:T(8,128)S(1)}, u32[]{:S(2)}, u32[]{:S(2)}) collective-permute-start(f32[80,768]{1,0:T(8,128)S(1)} %fusion.19), channel_id=1, source_target_pairs={{0,4},{4,0},{1,5},{5,1},{2,6},{6,2},{3,7},{7,3},{8,12},{12,8},{9,1... | collective-permute-start | bytes 737288 | tf_op jit(solution)/shard_map/ppermute | solution.py:91
  116.0 1.1 collective-permute-done.4
  117.1 0.2 fusion.11
  117.3 1.9 collective-permute-start.5
  119.2 13.2 %collective-permute-done.5 = bf16[80,768]{1,0:T(8,128)(2,1)S(1)} collective-permute-done((bf16[80,768]{1,0:T(8,128)(2,1)S(1)}, bf16[80,768]{1,0:T(8,128)(2,1)S(1)}, u32[]{:S(2)}, u32[]{:S(2)}) %collective-permute-start.5) | collective-permute-done | bytes 122912 | tf_op jit(solution)/shard_map/ppermute | solution.py:91
  132.5 2.1 collective-permute-start.6
  134.6 11.7 %collective-permute-done.6 = bf16[160,768]{1,0:T(8,128)(2,1)S(1)} collective-permute-done((bf16[160,768]{1,0:T(8,128)(2,1)S(1)}, bf16[160,768]{1,0:T(8,128)(2,1)S(1)}, u32[]{:S(2)}, u32[]{:S(2)}) %collective-permute-start.6) | collective-permute-done | bytes 245792 | tf_op jit(solution)/shard_map/ppermute | solution.py:91
  146.3 1.9 collective-permute-start.7
  148.2 12.3 %collective-permute-done.7.high = bf16[320,768]{1,0:T(8,128)(2,1)S(1)} collective-permute-done((bf16[320,768]{1,0:T(8,128)(2,1)S(1)}, bf16[320,768]{1,0:T(8,128)(2,1)S(1)}, u32[]{:S(2)}, u32[]{:S(2)}) %collective-permute-start.7) | collective-permute-done | bytes 491552 | tf_op jit(solution)/shard_map/ppermute | solution.py:91
  160.5 1.1 pad_maximum_fusion
  161.6 2.9 %shard_map.76 = bf16[8,80,768]{2,1,0:T(8,128)(2,1)} custom-call(s32[2]{0:T(128)S(1)} %pad_add_fusion.place, bf16[320,768]{1,0:T(8,128)(2,1)S(1)} %pad_maximum_fusion.1.low, bf16[320,768]{1,0:T(8,128)(2,1)S(1)} %collective-permute-done.7.high, bf16[2,768,384]{2,1,0:T(8,128)(2,1)S(1)} %bitcast.8, bf16[768,768]{1,0:T(8,128)(2,1)S(1)} %copy-done.3), custom_call_target="tpu_custom_call" | custom-call | flops 754974720 | bytes 6000000 | tf_op jit(solution)/shard_map/pallas_call | solution.py:80
  164.5 6.0 %all-to-all-start.1 = ((bf16[16,40,768]{2,1,0:T(8,128)(2,1)}), bf16[16,40,768]{2,1,0:T(8,128)(2,1)S(1)}, u32[]{:S(2)}, u32[]{:S(2)}) async-start(bf16[16,40,768]{2,1,0:T(8,128)(2,1)} %bitcast.5), calls=%async_computation.1 | async-start | bytes 1966080 | tf_op jit(solution)/shard_map/all_to_all | solution.py:144
  170.5 0.0 all-gather.13.cloned.1.call-start
  170.6 0.5 all-gather.13.cloned.1.call-update
  171.1 14.0 %all-to-all-done.1 = bf16[16,40,768]{2,1,0:T(8,128)(2,1)S(1)} async-done(((bf16[16,40,768]{2,1,0:T(8,128)(2,1)}), bf16[16,40,768]{2,1,0:T(8,128)(2,1)S(1)}, u32[]{:S(2)}, u32[]{:S(2)}) %all-to-all-start.1) | async-done | bytes 983072 | tf_op jit(solution)/shard_map/all_to_all | solution.py:144
  185.1 0.1 convert_reduce_fusion
  185.3 10.4 %collective-permute-start.8 = (bf16[20,768]{1,0:T(8,128)(2,1)S(1)}, bf16[20,768]{1,0:T(8,128)(2,1)S(1)}, u32[]{:S(2)}, u32[]{:S(2)}) collective-permute-start(bf16[20,768]{1,0:T(8,128)(2,1)S(1)} %slice.119), channel_id=1, source_target_pairs={{0,32},{32,0},{1,33},{33,1},{2,34},{34,2},{3,35},{35,3},{4,36},{36... | collective-permute-start | bytes 92168 | tf_op jit(solution)/shard_map/ppermute | solution.py:91
  195.7 3.0 %collective-permute-done.8 = bf16[20,768]{1,0:T(8,128)(2,1)S(1)} collective-permute-done((bf16[20,768]{1,0:T(8,128)(2,1)S(1)}, bf16[20,768]{1,0:T(8,128)(2,1)S(1)}, u32[]{:S(2)}, u32[]{:S(2)}) %collective-permute-start.8) | collective-permute-done | bytes 30752 | tf_op jit(solution)/shard_map/ppermute | solution.py:91
  198.8 6.3 %collective-permute-start.9 = (f32[10,768]{1,0:T(8,128)S(1)}, f32[10,768]{1,0:T(8,128)S(1)}, u32[]{:S(2)}, u32[]{:S(2)}) collective-permute-start(f32[10,768]{1,0:T(8,128)S(1)} %slice_select_fusion), channel_id=1, source_target_pairs={{0,4},{4,0},{1,5},{5,1},{2,6},{6,2},{3,7},{7,3},{8,12},{12,8},{9,1... | collective-permute-start | bytes 92168 | tf_op jit(solution)/shard_map/ppermute | solution.py:91
  205.1 0.9 collective-permute-done.9
  206.0 0.6 add_convert_fusion.1
  206.6 1.6 fusion.22
  208.3 3.2 %fusion.2 = f32[768,384]{1,0:T(8,128)} fusion(bf16[1280,768]{1,0:T(8,128)(2,1)} %all-gather.13.cloned.1.call-done, bf16[640,768]{1,0:T(8,128)(2,1)S(1)} %get-tuple-element.11, s32[]{:T(128)S(6)} %select_n.44), kind=kOutput, calls=%fused_computation.3 | convolution fusion | flops 377487360 | bytes 2654212 | tf_op jit(solution)/shard_map/dot_general | solution.py:153
  211.5 1.7 fusion
  (26 shorter events, 0.3 us)
Async XLA Ops:
  7.2 44.4 %all-gather.11.cloned.1.call-start = ((), (), s32[]{:S(2)}) async-start(), calls=%async_computation.3 | async-start | bytes 1769472 | tf_op jit(solution)/shard_map/all_gather | solution.py:105
  7.9 51.8 %all-gather.9.cloned.1.call-start = ((), (), s32[]{:S(2)}) async-start(), calls=%async_computation.2 | async-start | bytes 1769472 | tf_op jit(solution)/shard_map/all_gather | solution.py:106
  17.9 13.4 %collective-permute-start = (bf16[20,768]{1,0:T(8,128)(2,1)S(1)}, bf16[20,768]{1,0:T(8,128)(2,1)S(1)}, u32[]{:S(2)}, u32[]{:S(2)}) collective-permute-start(bf16[20,768]{1,0:T(8,128)(2,1)S(1)} %slice_select_fusion.1), channel_id=1, source_target_pairs={{0,32},{32,0},{1,33},{33,1},{2,34},{34,2},{3,35},{35,3},{4,36},{36... | collective-permute-start | bytes 92168 | tf_op jit(solution)/shard_map/ppermute | solution.py:91
  32.3 19.3 %all-to-all-start = ((bf16[16,40,768]{2,1,0:T(8,128)(2,1)}), bf16[16,40,768]{2,1,0:T(8,128)(2,1)S(1)}, u32[]{:S(2)}, u32[]{:S(2)}) async-start(bf16[16,40,768]{2,1,0:T(8,128)(2,1)} %broadcast_in_dim.2), calls=%async_computation | async-start | bytes 1966080 | tf_op jit(solution)/shard_map/all_to_all | solution.py:107
  37.2 169.4 %all-gather.15.cloned.1.call-start = ((), (), s32[]{:S(2)}) async-start(), calls=%async_computation.5 | async-start | bytes 2949120 | tf_op jit(solution)/shard_map/all_gather | solution.py:142
  59.7 1.3 copy-start
  61.0 1.3 copy-start.2
  65.0 14.5 %collective-permute-start.1 = (bf16[320,768]{1,0:T(8,128)(2,1)S(1)}, bf16[320,768]{1,0:T(8,128)(2,1)S(1)}, u32[]{:S(2)}, u32[]{:S(2)}) collective-permute-start(bf16[320,768]{1,0:T(8,128)(2,1)S(1)} %get-tuple-element.8), channel_id=1, source_target_pairs={{0,64},{64,0},{1,65},{65,1},{2,66},{66,2},{3,67},{67,3},{4,68},{68... | collective-permute-start | bytes 1474568 | tf_op jit(solution)/shard_map/ppermute | solution.py:91
  79.6 15.9 %collective-permute-start.2 = (bf16[160,768]{1,0:T(8,128)(2,1)S(1)}, bf16[160,768]{1,0:T(8,128)(2,1)S(1)}, u32[]{:S(2)}, u32[]{:S(2)}) collective-permute-start(bf16[160,768]{1,0:T(8,128)(2,1)S(1)} %get-tuple-element.12), channel_id=1, source_target_pairs={{0,128},{128,0},{1,129},{129,1},{2,130},{130,2},{3,131},{131,3},{4... | collective-permute-start | bytes 737288 | tf_op jit(solution)/shard_map/ppermute | solution.py:91
  95.6 17.9 %collective-permute-start.3 = (bf16[80,768]{1,0:T(8,128)(2,1)S(1)}, bf16[80,768]{1,0:T(8,128)(2,1)S(1)}, u32[]{:S(2)}, u32[]{:S(2)}) collective-permute-start(bf16[80,768]{1,0:T(8,128)(2,1)S(1)} %fusion.18), channel_id=1, source_target_pairs={{0,256},{256,0},{1,257},{257,1},{2,258},{258,2},{3,259},{259,3},{4... | collective-permute-start | bytes 368648 | tf_op jit(solution)/shard_map/ppermute | solution.py:91
  113.5 3.5 %collective-permute-start.4 = (f32[80,768]{1,0:T(8,128)S(1)}, f32[80,768]{1,0:T(8,128)S(1)}, u32[]{:S(2)}, u32[]{:S(2)}) collective-permute-start(f32[80,768]{1,0:T(8,128)S(1)} %fusion.19), channel_id=1, source_target_pairs={{0,4},{4,0},{1,5},{5,1},{2,6},{6,2},{3,7},{7,3},{8,12},{12,8},{9,1... | collective-permute-start | bytes 737288 | tf_op jit(solution)/shard_map/ppermute | solution.py:91
  117.3 15.2 %collective-permute-start.5 = (bf16[80,768]{1,0:T(8,128)(2,1)S(1)}, bf16[80,768]{1,0:T(8,128)(2,1)S(1)}, u32[]{:S(2)}, u32[]{:S(2)}) collective-permute-start(bf16[80,768]{1,0:T(8,128)(2,1)S(1)} %fusion.11), channel_id=1, source_target_pairs={{0,256},{256,0},{1,257},{257,1},{2,258},{258,2},{3,259},{259,3},{4... | collective-permute-start | bytes 368648 | tf_op jit(solution)/shard_map/ppermute | solution.py:91
  132.5 29.1 %copy-start.1 = (bf16[1536,384]{1,0:T(8,128)(2,1)S(1)}, bf16[1536,384]{1,0:T(8,128)(2,1)}, u32[]{:S(2)}) copy-start(bf16[1536,384]{1,0:T(8,128)(2,1)} %all-gather.11.cloned.1.call-done) | copy-start | bytes 3538948
  132.5 29.1 %copy-start.3 = (bf16[768,768]{1,0:T(8,128)(2,1)S(1)}, bf16[768,768]{1,0:T(8,128)(2,1)}, u32[]{:S(2)}) copy-start(bf16[768,768]{1,0:T(8,128)(2,1)} %all-gather.9.cloned.1.call-done.b) | copy-start | bytes 3538948
  132.5 13.7 %collective-permute-start.6 = (bf16[160,768]{1,0:T(8,128)(2,1)S(1)}, bf16[160,768]{1,0:T(8,128)(2,1)S(1)}, u32[]{:S(2)}, u32[]{:S(2)}) collective-permute-start(bf16[160,768]{1,0:T(8,128)(2,1)S(1)} %pad_maximum_fusion.2), channel_id=1, source_target_pairs={{0,128},{128,0},{1,129},{129,1},{2,130},{130,2},{3,131},{131,3},{4... | collective-permute-start | bytes 737288 | tf_op jit(solution)/shard_map/ppermute | solution.py:91
  146.3 14.2 %collective-permute-start.7 = (bf16[320,768]{1,0:T(8,128)(2,1)S(1)}, bf16[320,768]{1,0:T(8,128)(2,1)S(1)}, u32[]{:S(2)}, u32[]{:S(2)}) collective-permute-start(bf16[320,768]{1,0:T(8,128)(2,1)S(1)} %pad_maximum_fusion.1.low), channel_id=1, source_target_pairs={{0,64},{64,0},{1,65},{65,1},{2,66},{66,2},{3,67},{67,3},{4,68},{68... | collective-permute-start | bytes 1474568 | tf_op jit(solution)/shard_map/ppermute | solution.py:91
  164.5 41.5 %copy-start.5 = (bf16[10,768]{1,0:T(8,128)(2,1)S(1)}, bf16[10,768]{1,0:T(8,128)(2,1)}, u32[]{:S(2)}) copy-start(bf16[10,768]{1,0:T(8,128)(2,1)} %param.7) | copy-start | bytes 46084
  164.5 41.5 %copy-start.6 = (bf16[10,768]{1,0:T(8,128)(2,1)S(1)}, bf16[10,768]{1,0:T(8,128)(2,1)}, u32[]{:S(2)}) copy-start(bf16[10,768]{1,0:T(8,128)(2,1)} %param.4) | copy-start | bytes 46084
  164.5 20.6 %all-to-all-start.1 = ((bf16[16,40,768]{2,1,0:T(8,128)(2,1)}), bf16[16,40,768]{2,1,0:T(8,128)(2,1)S(1)}, u32[]{:S(2)}, u32[]{:S(2)}) async-start(bf16[16,40,768]{2,1,0:T(8,128)(2,1)} %bitcast.5), calls=%async_computation.1 | async-start | bytes 1966080 | tf_op jit(solution)/shard_map/all_to_all | solution.py:144
  170.5 37.8 %all-gather.13.cloned.1.call-start = ((), (), s32[]{:S(2)}) async-start(), calls=%async_computation.4 | async-start | bytes 2949120 | tf_op jit(solution)/shard_map/all_gather | solution.py:123
  185.3 13.4 %collective-permute-start.8 = (bf16[20,768]{1,0:T(8,128)(2,1)S(1)}, bf16[20,768]{1,0:T(8,128)(2,1)S(1)}, u32[]{:S(2)}, u32[]{:S(2)}) collective-permute-start(bf16[20,768]{1,0:T(8,128)(2,1)S(1)} %slice.119), channel_id=1, source_target_pairs={{0,32},{32,0},{1,33},{33,1},{2,34},{34,2},{3,35},{35,3},{4,36},{36... | collective-permute-start | bytes 92168 | tf_op jit(solution)/shard_map/ppermute | solution.py:91
  198.8 7.2 %collective-permute-start.9 = (f32[10,768]{1,0:T(8,128)S(1)}, f32[10,768]{1,0:T(8,128)S(1)}, u32[]{:S(2)}, u32[]{:S(2)}) collective-permute-start(f32[10,768]{1,0:T(8,128)S(1)} %slice_select_fusion), channel_id=1, source_target_pairs={{0,4},{4,0},{1,5},{5,1},{2,6},{6,2},{3,7},{7,3},{8,12},{12,8},{9,1... | collective-permute-start | bytes 92168 | tf_op jit(solution)/shard_map/ppermute | solution.py:91
  208.3 3.2 %copy-start.4 = (bf16[1280,768]{1,0:T(8,128)(2,1)S(1)}, bf16[1280,768]{1,0:T(8,128)(2,1)}, u32[]{:S(2)}) copy-start(bf16[1280,768]{1,0:T(8,128)(2,1)} %all-gather.13.cloned.1.call-done) | copy-start | bytes 5898244
Sparse Core Ops, SparseCore 0:
  10.1 26.4 all-gather.10
  38.7 21.0 all-gather.8
  161.7 21.5 all-gather.14
  185.8 22.1 all-gather.12

commit v2 on v0

v2 whole, which is shorter than its diff:
```python
import jax
import jax.numpy as jnp
from jax import lax
from jax.experimental import pallas as pl
from jax.experimental.pallas import tpu as pltpu
from jax.sharding import Mesh
from jax.sharding import PartitionSpec as P

ROW = ("za", "zb", "zc")
QUAD = ("zb", "zc")
CD = ("zhi", "x", "core", "y")
XY = ("x", "y")
CHIPS = ("zhi", "core")
SWAP = [(0, 1), (1, 0)]
F32 = jnp.float32
BF16 = jnp.bfloat16
NT = (((1,), (1,)), ((), ()))
TN = (((0,), (0,)), ((), ()))


def gelu_value(h):
    inner = 0.7978845608 * (h + 0.044715 * h * h * h)
    return 0.5 * h * (1.0 + jnp.tanh(inner))


def gelu_slope(h):
    inner = 0.7978845608 * (h + 0.044715 * h * h * h)
    t = jnp.tanh(inner)
    return 0.5 * (1.0 + t) + 0.5 * h * (1.0 - t * t) * 0.7978845608 * (1.0 + 3.0 * 0.044715 * h * h)


def dot(left, right, dims=(((1,), (0,)), ((), ()))):
    return lax.dot_general(left, right, dims, preferred_element_type=F32)


def first_kernel(core, x, own_in, got_in, own_out, got_out, out):
    width = own_in.shape[1]

    @pl.when(core[0] == 0)
    def _():
        out[:, :width] = dot(x[...], own_in[...]).astype(BF16)
        out[:, width:] = dot(x[...], got_in[...]).astype(BF16)

    @pl.when(core[0] == 1)
    def _():
        out[:, :width] = dot(x[...], got_out[...], NT).astype(BF16)
        out[:, width:] = dot(x[...], own_out[...], NT).astype(BF16)


def second_kernel(core, g, own_in, got_in, own_out, got_out, out, give):
    width = own_in.shape[1]

    @pl.when(core[0] == 0)
    def _():
        out[...] = (dot(g[:, :width], own_out[...]) + dot(g[:, width:], got_out[...])).astype(BF16)
        give[...] = g[:, width:]

    @pl.when(core[0] == 1)
    def _():
        out[...] = (dot(g[:, :width], got_in[...], NT) + dot(g[:, width:], own_in[...], NT)).astype(BF16)
        give[...] = g[:, :width]


def grads_kernel(core, x, y, g, k, in_grad, out_grad):
    width = k.shape[1]

    @pl.when(core[0] == 0)
    def _():
        in_grad[...] = dot(x[...], k[...], TN)
        out_grad[...] = dot(g[:, :width], y[...], TN)

    @pl.when(core[0] == 1)
    def _():
        in_grad[...] = dot(y[...], g[:, width:], TN)
        out_grad[...] = dot(k[...], x[...], TN)


def call(kernel, outs, core, *arrays):
    whole = pl.BlockSpec(memory_space=pltpu.VMEM)
    return pl.pallas_call(
        kernel,
        out_shape=outs,
        in_specs=[pl.BlockSpec(memory_space=pltpu.SMEM)] + [whole] * len(arrays),
        out_specs=jax.tree.map(lambda _: whole, outs),
        compiler_params=pltpu.CompilerParams(vmem_limit_bytes=40 * 1024 * 1024),
        cost_estimate=pl.CostEstimate(flops=2 * 640 * 768 * 768, bytes_accessed=5_000_000, transcendentals=0),
    )(core, *arrays)


def swap(x, axis):
    return lax.ppermute(x, axis, SWAP)


def body(tokens, in_weight, out_weight, cotangent):
    kept, feats = tokens.shape
    width = in_weight.shape[1]
    core, zhi = lax.axis_index("core"), lax.axis_index("zhi")
    is_first = core == 0
    low = lax.axis_index("za") == 0
    place = core.astype(jnp.int32).reshape(1)
    spread, four = 16, 4 * kept
    count = spread * four
    eighth = count // 8
    struct = jax.ShapeDtypeStruct

    both = lax.all_gather(jnp.concatenate([tokens, cotangent], axis=1), CHIPS, tiled=True)
    group = jnp.where(is_first, both[:, :feats], both[:, feats:])
    block = jnp.broadcast_to(group[None], (spread,) + group.shape)
    x = lax.all_to_all(block, XY, 0, 0, tiled=True).reshape(count, feats)
    weights = (in_weight, swap(in_weight, "core"), out_weight, swap(out_weight, "core"))

    part = call(first_kernel, struct((count, 2 * width), BF16), place, x, *weights)
    parts = lax.all_to_all(part.reshape(4, count // 4, 2 * width), QUAD, 0, 0, tiled=True)
    near = jnp.sum(parts.astype(F32), axis=0)
    sent = lax.all_gather(jnp.where(low, near[eighth:], near[:eighth]).astype(BF16), "za")
    full = jnp.where(low, near[:eighth], near[eighth:]) + jnp.where(low, sent[1], sent[0]).astype(F32)
    hidden = lax.all_gather(full.astype(BF16), "core")[0].astype(F32)
    shard = jnp.where(is_first, gelu_value(full), full * gelu_slope(hidden)).astype(BF16)
    shard = lax.all_gather(shard, "za", tiled=True)
    g = lax.all_gather(shard, QUAD, tiled=True)

    shapes = (struct((count, feats), BF16), struct((count, width), BF16))
    out, give = call(second_kernel, shapes, place, g, *weights)
    parts = lax.all_to_all(out.reshape(spread, four, feats), XY, 0, 0, tiled=True)
    y = swap(x, "core")
    k = swap(give, "core")
    shapes = (struct((feats, width), F32), struct((width, feats), F32))
    in_grad, out_grad = call(grads_kernel, shapes, place, x, y, g, k)
    sums = jnp.sum(parts.astype(F32), axis=0).astype(BF16)
    sums, in_grad, out_grad = lax.optimization_barrier((sums, in_grad, out_grad))
    sums = lax.all_gather(sums, CHIPS).reshape(2, 2, 4, kept, feats)
    sums = lax.dynamic_index_in_dim(sums, 2 * zhi + core, axis=2, keepdims=False).astype(F32)
    sums = sums[0] + sums[1]
    mixed = (tokens.astype(F32) + sums[0]).astype(BF16)
    token_grad = (cotangent.astype(F32) + sums[1]).astype(BF16)
    return (mixed, token_grad, in_grad, out_grad)


def solution(mesh):
    fine = Mesh(mesh.devices.reshape(2, 2, 2, 2, 4, 2, 4), ROW + CD)
    return jax.shard_map(
        body,
        mesh=fine,
        in_specs=(P(CD, ROW), P(ROW, CD), P(CD, ROW), P(CD, ROW)),
        out_specs=(P(CD, ROW), P(CD, ROW), P(ROW, CD), P(CD, ROW)),
        check_vma=False,
    )
```

time: 1810 us -> 171 us (0.09)
  waiting for transfers between devices: 1210 us -> 35.7 us
  blocking collectives: 563 us -> 92.1 us
  starting transfers between devices: 0.08 us -> 26.3 us
    unnamed x3 -> x0, waiting for transfers between devices: 1070 us -> none
    all_gather x2 -> x6, blocking collectives: 563 us -> 92.1 us  [the longest x1 21 us: body(): lax.all_gather(jnp.concatenate([tokens, cotangent], axis=1), CHIPS, tiled...]
    psum x1 -> x0, waiting for transfers between devices: 137 us -> none  [body(): lax.psum(partial_value.astype(jnp.bfloat16), 'row').astype(jnp.float32)]
    all_to_all x0 -> x3, waiting for transfers between devices: none -> 32.4 us  [the longest x1 19 us: body(): lax.all_to_all(part.reshape(4, count // 4, 2 * width), QUAD, 0, 0, tiled=...]
  transfers between devices with their start and end apart: 2 -> 7, of which waited for: 2 -> 5; matrix products, arithmetic and copies ran while one was open for 0% -> 0% of each run, Pallas kernels for 0% -> 3%
where the time goes in v2:
time: 171 us; the launch traced here: 170 us
  blocking collectives  92.1 us (54%)
  waiting for transfers between devices  35.7 us (21%)
  starting transfers between devices  26.3 us (15%)
  Pallas kernels  7.16 us (4%)
  local copies, waits for them, and re-layouts  4.78 us (3%)
  other arithmetic  3.25 us (2%)
    all_gather x1, blocking collectives, body(): lax.all_gather(jnp.concatenate([tokens, cotangent], axis=1), CHIPS, tiled...  21 us
    all_gather x1, blocking collectives, body(): g = lax.all_gather(shard, QUAD, tiled=True)  19.4 us
    all_to_all x1, waiting for transfers between devices, body(): lax.all_to_all(part.reshape(4, count // 4, 2 * width), QUAD, 0, 0, tiled=...  19 us
    all_gather x1, blocking collectives, body(): sums = lax.all_gather(sums, CHIPS).reshape(2, 2, 4, kept, feats)  17.6 us
    all_gather x1, blocking collectives, body(): lax.all_gather(jnp.where(low, near[eighth:], near[:eighth]).astype(BF16),...  17.1 us
    all_gather x1, blocking collectives, body(): shard = lax.all_gather(shard, 'za', tiled=True)  14.8 us
    ppermute x4, starting transfers between devices, swap(): return lax.ppermute(x, axis, SWAP)  12.9 us
    all_to_all x1, waiting for transfers between devices, body(): x = lax.all_to_all(block, XY, 0, 0, tiled=True).reshape(count, feats)  8.12 us
  transfers between devices with their start and end apart: 7, of which 5 were waited for; matrix products, arithmetic and copies ran while one was open for 0% of the time, Pallas kernels for 3%

profile of v2, /device:TPU:1, one launch (start us, length us, event | category | flops | bytes accessed | tf_op | source)
XLA Modules:
  0.0 170.1 jit_solution(7166235019713014139)
XLA Ops:
  0.6 0.8 maximum_bitcast_fusion
  1.4 21.0 %all-gather.3 = bf16[4,10,1536]{2,1,0:T(8,128)(2,1)S(1)} all-gather(bf16[1,10,1536]{2,1,0:T(8,128)(2,1)S(1)} %maximum_bitcast_fusion), channel_id=1, replica_groups=mesh['za'=2,'zb'=2,'zc'=2,'zhi'=2,'x'=4,'core'=2,'y'=4] {'zhi','core'}, dimensions={0}, use_global_device_ids=true | all-gather | bytes 153600 | tf_op jit(solution)/shard_map/all_gather | solution.py:106
  22.5 1.0 broadcast_in_dim.2
  23.5 0.0 copy-start
  23.5 5.2 %all-to-all-start = ((bf16[16,40,768]{2,1,0:T(8,128)(2,1)}), bf16[16,40,768]{2,1,0:T(8,128)(2,1)S(1)}, u32[]{:S(2)}, u32[]{:S(2)}) async-start(bf16[16,40,768]{2,1,0:T(8,128)(2,1)} %broadcast_in_dim.2), calls=%async_computation | async-start | bytes 1966080 | tf_op jit(solution)/shard_map/all_to_all | solution.py:109
  28.7 0.0 copy-done
  28.7 2.4 %collective-permute-start = (bf16[768,384]{1,0:T(8,128)(2,1)S(1)}, bf16[768,384]{1,0:T(8,128)(2,1)S(1)}, u32[]{:S(2)}, u32[]{:S(2)}) collective-permute-start(bf16[768,384]{1,0:T(8,128)(2,1)S(1)} %copy-done), channel_id=1, source_target_pairs={{0,4},{4,0},{1,5},{5,1},{2,6},{6,2},{3,7},{7,3},{8,12},{12,8},{9,1... | collective-permute-start | bytes 1769480 | tf_op jit(solution)/shard_map/ppermute | solution.py:91
  31.1 0.0 copy-done.1
  31.1 2.0 %collective-permute-start.1 = (bf16[384,768]{1,0:T(8,128)(2,1)S(1)}, bf16[384,768]{1,0:T(8,128)(2,1)S(1)}, u32[]{:S(2)}, u32[]{:S(2)}) collective-permute-start(bf16[384,768]{1,0:T(8,128)(2,1)S(1)} %copy-done.1), channel_id=1, source_target_pairs={{0,4},{4,0},{1,5},{5,1},{2,6},{6,2},{3,7},{7,3},{8,12},{12,8},{9,1... | collective-permute-start | bytes 1769480 | tf_op jit(solution)/shard_map/ppermute | solution.py:91
  33.1 0.0 collective-permute-done.got_in
  33.1 0.0 copy-start.2
  33.1 1.9 %collective-permute-done.1.got_out = bf16[384,768]{1,0:T(8,128)(2,1)S(1)} collective-permute-done((bf16[384,768]{1,0:T(8,128)(2,1)S(1)}, bf16[384,768]{1,0:T(8,128)(2,1)S(1)}, u32[]{:S(2)}, u32[]{:S(2)}) %collective-permute-start.1) | collective-permute-done | bytes 589856 | tf_op jit(solution)/shard_map/ppermute | solution.py:91
  35.0 0.8 copy-done.4
  35.8 8.1 %all-to-all-done = bf16[16,40,768]{2,1,0:T(8,128)(2,1)S(1)} async-done(((bf16[16,40,768]{2,1,0:T(8,128)(2,1)}), bf16[16,40,768]{2,1,0:T(8,128)(2,1)S(1)}, u32[]{:S(2)}, u32[]{:S(2)}) %all-to-all-start) | async-done | bytes 983072 | tf_op jit(solution)/shard_map/all_to_all | solution.py:109
  44.0 1.1 copy-done.5
  45.0 2.1 %shard_map.75 = bf16[640,768]{1,0:T(8,128)(2,1)} custom-call(s32[1]{0:T(128)} %bitcast.core, bf16[640,768]{1,0:T(8,128)(2,1)S(1)} %bitcast.20, bf16[768,384]{1,0:T(8,128)(2,1)S(1)} %copy-done, bf16[768,384]{1,0:T(8,128)(2,1)S(1)} %collective-permute-done.got_in, bf16[384,768]{1,0:T(8,128)(2,1)S(1)} %copy-done.1, bf16[384,768]{1,0:T(8,128)(2,1)S(1)} %copy-done.5), custom_call_target="tpu_custom_call" | custom-call | flops 754974720 | bytes 5000000 | tf_op jit(solution)/shard_map/pallas_call | solution.py:80
  47.1 0.0 copy-done.2
  47.2 3.5 %all-to-all-start.1 = ((bf16[4,160,768]{2,1,0:T(8,128)(2,1)}), bf16[4,160,768]{2,1,0:T(8,128)(2,1)S(1)}, u32[]{:S(2)}, u32[]{:S(2)}) async-start(bf16[4,160,768]{2,1,0:T(8,128)(2,1)} %bitcast.3), calls=%async_computation.1 | async-start | bytes 1966080 | tf_op jit(solution)/shard_map/all_to_all | solution.py:113
  50.7 4.8 %collective-permute-start.2 = (bf16[640,768]{1,0:T(8,128)(2,1)S(1)}, bf16[640,768]{1,0:T(8,128)(2,1)}, u32[]{:S(2)}, u32[]{:S(2)}) collective-permute-start(bf16[640,768]{1,0:T(8,128)(2,1)S(1)} %bitcast.21), channel_id=1, source_target_pairs={{0,4},{4,0},{1,5},{5,1},{2,6},{6,2},{3,7},{7,3},{8,12},{12,8},{9,1... | collective-permute-start | bytes 2949128 | tf_op jit(solution)/shard_map/ppermute | solution.py:91
  55.5 19.0 %all-to-all-done.1 = bf16[4,160,768]{2,1,0:T(8,128)(2,1)S(1)} async-done(((bf16[4,160,768]{2,1,0:T(8,128)(2,1)}), bf16[4,160,768]{2,1,0:T(8,128)(2,1)S(1)}, u32[]{:S(2)}, u32[]{:S(2)}) %all-to-all-start.1) | async-done | bytes 983072 | tf_op jit(solution)/shard_map/all_to_all | solution.py:113
  74.4 0.1 convert_reduce_fusion
  74.6 17.1 %all-gather = bf16[160,768]{1,0:T(8,128)(2,1)S(1)} all-gather(bf16[80,768]{1,0:T(8,128)(2,1)S(1)} %select_convert_fusion), channel_id=2, replica_groups=mesh['za'=2,'zb'=2,'zc'=2,'zhi'=2,'x'=4,'core'=2,'y'=4] {'za'}, dimensions={0}, use_global_device_ids=true | all-gather | bytes 368640 | tf_op jit(solution)/shard_map/all_gather | solution.py:115
  91.7 0.1 fusion.19
  91.7 0.0 copy-start.3
  91.8 0.0 copy-start.6
  91.8 2.2 %all-gather.1 = bf16[160,768]{1,0:T(8,128)(2,1)S(1)} all-gather(bf16[80,768]{1,0:T(8,128)(2,1)S(1)} %get-tuple-element.18), channel_id=3, replica_groups=mesh['za'=2,'zb'=2,'zc'=2,'zhi'=2,'x'=4,'core'=2,'y'=4] {'core'}, dimensions={0}, use_global_device_ids=true | all-gather | bytes 368640 | tf_op jit(solution)/shard_map/all_gather | solution.py:117
  94.0 0.3 fusion.5
  94.3 14.8 %all_gather.32 = bf16[160,768]{1,0:T(8,128)(2,1)S(1)} all-gather(bf16[80,768]{1,0:T(8,128)(2,1)S(1)} %fusion.5), channel_id=1, replica_groups=mesh['za'=2,'zb'=2,'zc'=2,'zhi'=2,'x'=4,'core'=2,'y'=4] {'za'}, dimensions={0}, use_global_device_ids=true | all-gather | bytes 368640 | tf_op jit(solution)/shard_map/all_gather | solution.py:119
  109.1 19.4 %all_gather.33.g = bf16[640,768]{1,0:T(8,128)(2,1)S(1)} all-gather(bf16[160,768]{1,0:T(8,128)(2,1)S(1)} %all_gather.32), channel_id=1, replica_groups=mesh['za'=2,'zb'=2,'zc'=2,'zhi'=2,'x'=4,'core'=2,'y'=4] {'zb','zc'}, dimensions={0}, use_global_device_ids=true | all-gather | bytes 1228800 | tf_op jit(solution)/shard_map/all_gather | solution.py:120
  128.4 0.0 copy-done.3
  128.4 0.0 copy-done.6
  128.4 1.2 shard_map.76
  129.6 0.0 copy-start.7
  129.6 0.9 copy-done.7
  130.6 0.8 copy-done.8
  131.4 4.6 %all-to-all-start.2 = ((bf16[16,40,768]{2,1,0:T(8,128)(2,1)}), bf16[16,40,768]{2,1,0:T(8,128)(2,1)}, u32[]{:S(2)}, u32[]{:S(2)}) async-start(bf16[16,40,768]{2,1,0:T(8,128)(2,1)} %bitcast.23), calls=%async_computation.2 | async-start | bytes 1966080 | tf_op jit(solution)/shard_map/all_to_all | solution.py:124
  136.0 0.0 copy-done.9
  136.0 3.8 %collective-permute-start.3 = (bf16[640,384]{1,0:T(8,128)(2,1)S(1)}, bf16[640,384]{1,0:T(8,128)(2,1)S(1)}, u32[]{:S(2)}, u32[]{:S(2)}) collective-permute-start(bf16[640,384]{1,0:T(8,128)(2,1)S(1)} %copy-done.9), channel_id=1, source_target_pairs={{0,4},{4,0},{1,5},{5,1},{2,6},{6,2},{3,7},{7,3},{8,12},{12,8},{9,1... | collective-permute-start | bytes 1474568 | tf_op jit(solution)/shard_map/ppermute | solution.py:91
  139.8 0.0 collective-permute-done.2.y
  139.8 1.4 collective-permute-done.3.k
  141.3 3.8 %shard_map.77 = (f32[768,384]{1,0:T(8,128)}, f32[384,768]{1,0:T(8,128)}) custom-call(s32[1]{0:T(128)} %bitcast.core, bf16[640,768]{1,0:T(8,128)(2,1)S(1)} %bitcast.22, bf16[640,768]{1,0:T(8,128)(2,1)} %collective-permute-done.2.y, bf16[640,768]{1,0:T(8,128)(2,1)S(1)} %all_gather.33.g, bf16[640,384]{1,0:T(8,128)(2,1)S(1)} %collective-permute-done.3.k), custom_call_target="tpu_custom_call" | custom-call | flops 754974720 | bytes 5000000 | tf_op jit(solution)/shard_map/pallas_call | solution.py:80
  145.1 5.3 %all-to-all-done.2 = bf16[16,40,768]{2,1,0:T(8,128)(2,1)} async-done(((bf16[16,40,768]{2,1,0:T(8,128)(2,1)}), bf16[16,40,768]{2,1,0:T(8,128)(2,1)}, u32[]{:S(2)}, u32[]{:S(2)}) %all-to-all-start.2) | async-done | bytes 983072 | tf_op jit(solution)/shard_map/all_to_all | solution.py:124
  150.4 1.3 reduce_sum.22
  151.7 17.6 %all-gather.2 = bf16[160,768]{1,0:T(8,128)(2,1)S(1)} all-gather(bf16[40,768]{1,0:T(8,128)(2,1)S(1)} %reduce_sum.22), channel_id=4, replica_groups=mesh['za'=2,'zb'=2,'zc'=2,'zhi'=2,'x'=4,'core'=2,'y'=4] {'zhi','core'}, dimensions={0}, use_global_device_ids=true | all-gather | bytes 307200 | tf_op jit(solution)/shard_map/all_gather | solution.py:131
  169.3 0.1 reshape.43
  169.5 0.0 copy-done.10
  169.5 0.0 copy-done.11
  169.5 0.6 fusion.16
  (12 shorter events, 0.1 us)
Async XLA Ops:
  23.5 5.2 %copy-start = (bf16[768,384]{1,0:T(8,128)(2,1)S(1)}, bf16[768,384]{1,0:T(8,128)(2,1)}, u32[]{:S(2)}) copy-start(bf16[768,384]{1,0:T(8,128)(2,1)} %own_in.3) | copy-start | bytes 1769476
  23.5 7.6 %copy-start.1 = (bf16[384,768]{1,0:T(8,128)(2,1)S(1)}, bf16[384,768]{1,0:T(8,128)(2,1)}, u32[]{:S(2)}) copy-start(bf16[384,768]{1,0:T(8,128)(2,1)} %own_out.3) | copy-start | bytes 1769476
  23.5 20.4 %all-to-all-start = ((bf16[16,40,768]{2,1,0:T(8,128)(2,1)}), bf16[16,40,768]{2,1,0:T(8,128)(2,1)S(1)}, u32[]{:S(2)}, u32[]{:S(2)}) async-start(bf16[16,40,768]{2,1,0:T(8,128)(2,1)} %broadcast_in_dim.2), calls=%async_computation | async-start | bytes 1966080 | tf_op jit(solution)/shard_map/all_to_all | solution.py:109
  28.7 4.4 %collective-permute-start = (bf16[768,384]{1,0:T(8,128)(2,1)S(1)}, bf16[768,384]{1,0:T(8,128)(2,1)S(1)}, u32[]{:S(2)}, u32[]{:S(2)}) collective-permute-start(bf16[768,384]{1,0:T(8,128)(2,1)S(1)} %copy-done), channel_id=1, source_target_pairs={{0,4},{4,0},{1,5},{5,1},{2,6},{6,2},{3,7},{7,3},{8,12},{12,8},{9,1... | collective-permute-start | bytes 1769480 | tf_op jit(solution)/shard_map/ppermute | solution.py:91
  31.1 3.9 %collective-permute-start.1 = (bf16[384,768]{1,0:T(8,128)(2,1)S(1)}, bf16[384,768]{1,0:T(8,128)(2,1)S(1)}, u32[]{:S(2)}, u32[]{:S(2)}) collective-permute-start(bf16[384,768]{1,0:T(8,128)(2,1)S(1)} %copy-done.1), channel_id=1, source_target_pairs={{0,4},{4,0},{1,5},{5,1},{2,6},{6,2},{3,7},{7,3},{8,12},{12,8},{9,1... | collective-permute-start | bytes 1769480 | tf_op jit(solution)/shard_map/ppermute | solution.py:91
  33.1 14.0 %copy-start.2 = (bf16[768,384]{1,0:T(8,128)(2,1)}, bf16[768,384]{1,0:T(8,128)(2,1)S(1)}, u32[]{:S(2)}) copy-start(bf16[768,384]{1,0:T(8,128)(2,1)S(1)} %collective-permute-done.got_in) | copy-start | bytes 1769476
  35.0 0.8 copy-start.4
  44.0 1.1 copy-start.5
  47.2 27.3 %all-to-all-start.1 = ((bf16[4,160,768]{2,1,0:T(8,128)(2,1)}), bf16[4,160,768]{2,1,0:T(8,128)(2,1)S(1)}, u32[]{:S(2)}, u32[]{:S(2)}) async-start(bf16[4,160,768]{2,1,0:T(8,128)(2,1)} %bitcast.3), calls=%async_computation.1 | async-start | bytes 1966080 | tf_op jit(solution)/shard_map/all_to_all | solution.py:113
  50.7 89.1 %collective-permute-start.2 = (bf16[640,768]{1,0:T(8,128)(2,1)S(1)}, bf16[640,768]{1,0:T(8,128)(2,1)}, u32[]{:S(2)}, u32[]{:S(2)}) collective-permute-start(bf16[640,768]{1,0:T(8,128)(2,1)S(1)} %bitcast.21), channel_id=1, source_target_pairs={{0,4},{4,0},{1,5},{5,1},{2,6},{6,2},{3,7},{7,3},{8,12},{12,8},{9,1... | collective-permute-start | bytes 2949128 | tf_op jit(solution)/shard_map/ppermute | solution.py:91
  91.7 36.7 %copy-start.3 = (bf16[768,384]{1,0:T(8,128)(2,1)S(1)}, bf16[768,384]{1,0:T(8,128)(2,1)}, u32[]{:S(2)}) copy-start(bf16[768,384]{1,0:T(8,128)(2,1)} %copy-done.2) | copy-start | bytes 1769476
  91.8 36.7 %copy-start.6 = (bf16[384,768]{1,0:T(8,128)(2,1)S(1)}, bf16[384,768]{1,0:T(8,128)(2,1)}, u32[]{:S(2)}) copy-start(bf16[384,768]{1,0:T(8,128)(2,1)} %copy-done.4) | copy-start | bytes 1769476
  129.6 1.0 copy-start.7
  130.6 0.8 copy-start.8
  131.4 4.6 %copy-start.9 = (bf16[640,384]{1,0:T(8,128)(2,1)S(1)}, bf16[640,384]{1,0:T(8,128)(2,1)}, u32[]{:S(2)}) copy-start(bf16[640,384]{1,0:T(8,128)(2,1)} %copy-done.8) | copy-start | bytes 1474564
  131.4 19.0 %all-to-all-start.2 = ((bf16[16,40,768]{2,1,0:T(8,128)(2,1)}), bf16[16,40,768]{2,1,0:T(8,128)(2,1)}, u32[]{:S(2)}, u32[]{:S(2)}) async-start(bf16[16,40,768]{2,1,0:T(8,128)(2,1)} %bitcast.23), calls=%async_computation.2 | async-start | bytes 1966080 | tf_op jit(solution)/shard_map/all_to_all | solution.py:124
  136.0 5.3 %collective-permute-start.3 = (bf16[640,384]{1,0:T(8,128)(2,1)S(1)}, bf16[640,384]{1,0:T(8,128)(2,1)S(1)}, u32[]{:S(2)}, u32[]{:S(2)}) collective-permute-start(bf16[640,384]{1,0:T(8,128)(2,1)S(1)} %copy-done.9), channel_id=1, source_target_pairs={{0,4},{4,0},{1,5},{5,1},{2,6},{6,2},{3,7},{7,3},{8,12},{12,8},{9,1... | collective-permute-start | bytes 1474568 | tf_op jit(solution)/shard_map/ppermute | solution.py:91
  145.1 24.4 %copy-start.10 = (bf16[10,768]{1,0:T(8,128)(2,1)S(1)}, bf16[10,768]{1,0:T(8,128)(2,1)}, u32[]{:S(2)}) copy-start(bf16[10,768]{1,0:T(8,128)(2,1)} %param.7) | copy-start | bytes 46084
  145.1 24.4 %copy-start.11 = (bf16[10,768]{1,0:T(8,128)(2,1)S(1)}, bf16[10,768]{1,0:T(8,128)(2,1)}, u32[]{:S(2)}) copy-start(bf16[10,768]{1,0:T(8,128)(2,1)} %param.4) | copy-start | bytes 46084

commit v3 on v2

--- a/solution.py
+++ b/solution.py
@@ -33,18 +33,21 @@
     return lax.dot_general(left, right, dims, preferred_element_type=F32)
 
 
-def first_kernel(core, x, own_in, got_in, own_out, got_out, out):
+def first_kernel(place, x, own_in, got_in, own_out, got_out, out, rows):
     width = own_in.shape[1]
+    size = x.shape[2]
+    for q in range(x.shape[0]):
+        rows[size * q : size * (q + 1), :] = x[q, place[1]]
 
-    @pl.when(core[0] == 0)
+    @pl.when(place[0] == 0)
     def _():
-        out[:, :width] = dot(x[...], own_in[...]).astype(BF16)
-        out[:, width:] = dot(x[...], got_in[...]).astype(BF16)
+        out[:, :width] = dot(rows[...], own_in[...]).astype(BF16)
+        out[:, width:] = dot(rows[...], got_in[...]).astype(BF16)
 
-    @pl.when(core[0] == 1)
+    @pl.when(place[0] == 1)
     def _():
-        out[:, :width] = dot(x[...], got_out[...], NT).astype(BF16)
-        out[:, width:] = dot(x[...], own_out[...], NT).astype(BF16)
+        out[:, :width] = dot(rows[...], got_out[...], NT).astype(BF16)
+        out[:, width:] = dot(rows[...], own_out[...], NT).astype(BF16)
 
 
 def second_kernel(core, g, own_in, got_in, own_out, got_out, out, give):
@@ -75,13 +78,14 @@
         out_grad[...] = dot(k[...], x[...], TN)
 
 
-def call(kernel, outs, core, *arrays):
+def call(kernel, outs, core, *arrays, scratch=()):
     whole = pl.BlockSpec(memory_space=pltpu.VMEM)
     return pl.pallas_call(
         kernel,
         out_shape=outs,
         in_specs=[pl.BlockSpec(memory_space=pltpu.SMEM)] + [whole] * len(arrays),
         out_specs=jax.tree.map(lambda _: whole, outs),
+        scratch_shapes=scratch,
         compiler_params=pltpu.CompilerParams(vmem_limit_bytes=40 * 1024 * 1024),
         cost_estimate=pl.CostEstimate(flops=2 * 640 * 768 * 768, bytes_accessed=5_000_000, transcendentals=0),
     )(core, *arrays)
@@ -91,16 +95,19 @@
     return lax.ppermute(x, axis, SWAP)
 
 
+def tie(*arrays):
+    return lax.optimization_barrier(arrays)
+
+
 def body(tokens, in_weight, out_weight, cotangent):
     kept, feats = tokens.shape
     width = in_weight.shape[1]
-    core, zhi = lax.axis_index("core"), lax.axis_index("zhi")
+    core, zhi, za = lax.axis_index("core"), lax.axis_index("zhi"), lax.axis_index("za")
     is_first = core == 0
-    low = lax.axis_index("za") == 0
     place = core.astype(jnp.int32).reshape(1)
     spread, four = 16, 4 * kept
     count = spread * four
-    eighth = count // 8
+    half, eighth = count // 2, count // 8
     struct = jax.ShapeDtypeStruct
 
     both = lax.all_gather(jnp.concatenate([tokens, cotangent], axis=1), CHIPS, tiled=True)
@@ -109,11 +116,26 @@
     x = lax.all_to_all(block, XY, 0, 0, tiled=True).reshape(count, feats)
     weights = (in_weight, swap(in_weight, "core"), out_weight, swap(out_weight, "core"))
 
-    part = call(first_kernel, struct((count, 2 * width), BF16), place, x, *weights)
-    parts = lax.all_to_all(part.reshape(4, count // 4, 2 * width), QUAD, 0, 0, tiled=True)
-    near = jnp.sum(parts.astype(F32), axis=0)
-    sent = lax.all_gather(jnp.where(low, near[eighth:], near[:eighth]).astype(BF16), "za")
-    full = jnp.where(low, near[:eighth], near[eighth:]) + jnp.where(low, sent[1], sent[0]).astype(F32)
+    def terms(which):
+        out = call(
+            first_kernel,
+            struct((half, 2 * width), BF16),
+            jnp.stack([core, which]).astype(jnp.int32),
+            x.reshape(4, 2, eighth, feats),
+            *weights,
+            scratch=[pltpu.VMEM((half, feats), BF16)],
+        )
+        return out.reshape(4, eighth, 2 * width)
+
+    def exchange(blocks):
+        return lax.all_to_all(blocks, QUAD, 0, 0, tiled=True)
+
+    def total(parts):
+        return jnp.sum(parts.astype(F32), axis=0)
+
+    far, near, y = tie(exchange(terms(1 - za)), terms(za), swap(x, "core"))
+    came = swap(total(far).astype(BF16), "za")
+    full = total(exchange(near)) + came.astype(F32)
     hidden = lax.all_gather(full.astype(BF16), "core")[0].astype(F32)
     shard = jnp.where(is_first, gelu_value(full), full * gelu_slope(hidden)).astype(BF16)
     shard = lax.all_gather(shard, "za", tiled=True)
@@ -122,13 +144,11 @@
     shapes = (struct((count, feats), BF16), struct((count, width), BF16))
     out, give = call(second_kernel, shapes, place, g, *weights)
     parts = lax.all_to_all(out.reshape(spread, four, feats), XY, 0, 0, tiled=True)
-    y = swap(x, "core")
     k = swap(give, "core")
     shapes = (struct((feats, width), F32), struct((width, feats), F32))
     in_grad, out_grad = call(grads_kernel, shapes, place, x, y, g, k)
-    sums = jnp.sum(parts.astype(F32), axis=0).astype(BF16)
-    sums, in_grad, out_grad = lax.optimization_barrier((sums, in_grad, out_grad))
-    sums = lax.all_gather(sums, CHIPS).reshape(2, 2, 4, kept, feats)
+    parts, in_grad, out_grad = tie(parts, in_grad, out_grad)
+    sums = lax.all_gather(total(parts).astype(BF16), CHIPS).reshape(2, 2, 4, kept, feats)
     sums = lax.dynamic_index_in_dim(sums, 2 * zhi + core, axis=2, keepdims=False).astype(F32)
     sums = sums[0] + sums[1]
     mixed = (tokens.astype(F32) + sums[0]).astype(BF16)

time: 171 us -> 169 us (0.988)
  starting transfers between devices: 26.3 us -> 41.3 us
  blocking collectives: 92.1 us -> 80.4 us
  waiting for transfers between devices: 35.7 us -> 27.4 us
  Pallas kernels: 7.16 us -> 11.1 us
    all_gather x2 -> x1, blocking collectives: 34.7 us -> 17.5 us  [body(): lax.all_gather(total(parts).astype(BF16), CHIPS)]
    all_to_all x1 -> x2, waiting for transfers between devices: 19 us -> 9.72 us  [exchange(): return lax.all_to_all(blocks, QUAD, 0, 0, tiled=True)]
    ppermute x4 -> x5, starting transfers between devices: 12.9 us -> 20.3 us  [swap(): return lax.ppermute(x, axis, SWAP)]
    all_to_all x1 -> x2, starting transfers between devices: 3.51 us -> 8.72 us  [exchange(): return lax.all_to_all(blocks, QUAD, 0, 0, tiled=True)]
    all_gather x1, blocking collectives: 2.25 us -> 6.62 us  [body(): hidden = lax.all_gather(full.astype(BF16), 'core')[0].astype(F32)]
    pallas_call x3 -> x4, Pallas kernels: 7.16 us -> 11.1 us  [call(): pl.pallas_call(kernel, out_shape=outs, in_specs=[pl.BlockSpec(memory_spac...]
    all_to_all x1, starting transfers between devices: 4.6 us -> 7.07 us  [body(): lax.all_to_all(out.reshape(spread, four, feats), XY, 0, 0, tiled=True)]
    all_gather x1, blocking collectives: 14.8 us -> 17 us  [body(): shard = lax.all_gather(shard, 'za', tiled=True)]
  transfers between devices with their start and end apart: 7 -> 9, of which waited for: 5 -> 6; matrix products, arithmetic and copies ran while one was open for 0% -> 0% of each run, Pallas kernels for 3% -> 4%
where the time goes in v3:
time: 169 us; the launch traced here: 168 us
  blocking collectives  80.4 us (48%)
  starting transfers between devices  41.3 us (24%)
  waiting for transfers between devices  27.4 us (16%)
  Pallas kernels  11.1 us (7%)
  local copies, waits for them, and re-layouts  3.86 us (2%)
  other arithmetic  3.31 us (2%)
    all_gather x1, blocking collectives, body(): lax.all_gather(jnp.concatenate([tokens, cotangent], axis=1), CHIPS, tiled...  21 us
    ppermute x5, starting transfers between devices, swap(): return lax.ppermute(x, axis, SWAP)  20.3 us
    all_gather x1, blocking collectives, body(): g = lax.all_gather(shard, QUAD, tiled=True)  18.3 us
    all_gather x1, blocking collectives, body(): lax.all_gather(total(parts).astype(BF16), CHIPS)  17.5 us
    all_gather x1, blocking collectives, body(): shard = lax.all_gather(shard, 'za', tiled=True)  17 us
    pallas_call x4, Pallas kernels, call(): pl.pallas_call(kernel, out_shape=outs, in_specs=[pl.BlockSpec(memory_spac...  11.1 us
    all_to_all x2, waiting for transfers between devices, exchange(): return lax.all_to_all(blocks, QUAD, 0, 0, tiled=True)  9.72 us
    all_to_all x1, waiting for transfers between devices, body(): x = lax.all_to_all(block, XY, 0, 0, tiled=True).reshape(count, feats)  8.81 us
  transfers between devices with their start and end apart: 9, of which 6 were waited for; matrix products, arithmetic and copies ran while one was open for 0% of the time, Pallas kernels for 4%

profile of v3, /device:TPU:1, one launch (start us, length us, event | category | flops | bytes accessed | tf_op | source)
XLA Modules:
  0.0 168.2 jit_solution(623691500314007875)
XLA Ops:
  0.6 0.8 maximum_bitcast_fusion
  1.4 21.0 %all-gather.2 = bf16[4,10,1536]{2,1,0:T(8,128)(2,1)S(1)} all-gather(bf16[1,10,1536]{2,1,0:T(8,128)(2,1)S(1)} %maximum_bitcast_fusion), channel_id=1, replica_groups=mesh['za'=2,'zb'=2,'zc'=2,'zhi'=2,'x'=4,'core'=2,'y'=4] {'zhi','core'}, dimensions={0}, use_global_device_ids=true | all-gather | bytes 153600 | tf_op jit(solution)/shard_map/all_gather | solution.py:113
  22.5 1.0 broadcast_in_dim.2
  23.5 0.0 copy-start
  23.5 5.2 %all-to-all-start = ((bf16[16,40,768]{2,1,0:T(8,128)(2,1)}), bf16[16,40,768]{2,1,0:T(8,128)(2,1)S(1)}, u32[]{:S(2)}, u32[]{:S(2)}) async-start(bf16[16,40,768]{2,1,0:T(8,128)(2,1)} %broadcast_in_dim.2), calls=%async_computation | async-start | bytes 1966080 | tf_op jit(solution)/shard_map/all_to_all | solution.py:116
  28.7 0.0 copy-done
  28.7 2.4 %collective-permute-start = (bf16[768,384]{1,0:T(8,128)(2,1)S(1)}, bf16[768,384]{1,0:T(8,128)(2,1)S(1)}, u32[]{:S(2)}, u32[]{:S(2)}) collective-permute-start(bf16[768,384]{1,0:T(8,128)(2,1)S(1)} %copy-done), channel_id=1, source_target_pairs={{0,4},{4,0},{1,5},{5,1},{2,6},{6,2},{3,7},{7,3},{8,12},{12,8},{9,1... | collective-permute-start | bytes 1769480 | tf_op jit(solution)/shard_map/ppermute | solution.py:95
  31.1 0.0 copy-done.1
  31.1 2.0 %collective-permute-start.1 = (bf16[384,768]{1,0:T(8,128)(2,1)S(1)}, bf16[384,768]{1,0:T(8,128)(2,1)}, u32[]{:S(2)}, u32[]{:S(2)}) collective-permute-start(bf16[384,768]{1,0:T(8,128)(2,1)S(1)} %copy-done.1), channel_id=1, source_target_pairs={{0,4},{4,0},{1,5},{5,1},{2,6},{6,2},{3,7},{7,3},{8,12},{12,8},{9,1... | collective-permute-start | bytes 1769480 | tf_op jit(solution)/shard_map/ppermute | solution.py:95
  33.1 0.1 pad_add_fusion
  33.2 0.0 collective-permute-done.got_in
  33.2 2.0 %collective-permute-done.1.got_out = bf16[384,768]{1,0:T(8,128)(2,1)} collective-permute-done((bf16[384,768]{1,0:T(8,128)(2,1)S(1)}, bf16[384,768]{1,0:T(8,128)(2,1)}, u32[]{:S(2)}, u32[]{:S(2)}) %collective-permute-start.1) | collective-permute-done | bytes 589856 | tf_op jit(solution)/shard_map/ppermute | solution.py:95
  35.1 8.8 %all-to-all-done = bf16[16,40,768]{2,1,0:T(8,128)(2,1)S(1)} async-done(((bf16[16,40,768]{2,1,0:T(8,128)(2,1)}), bf16[16,40,768]{2,1,0:T(8,128)(2,1)S(1)}, u32[]{:S(2)}, u32[]{:S(2)}) %all-to-all-start) | async-done | bytes 983072 | tf_op jit(solution)/shard_map/all_to_all | solution.py:116
  44.0 2.6 %shard_map.75 = bf16[320,768]{1,0:T(8,128)(2,1)} custom-call(s32[2]{0:T(128)S(1)} %get-tuple-element.26.place, bf16[4,2,80,768]{3,2,1,0:T(8,128)(2,1)S(1)} %bitcast.24, bf16[768,384]{1,0:T(8,128)(2,1)S(1)} %copy-done, bf16[768,384]{1,0:T(8,128)(2,1)S(1)} %collective-permute-done.got_in, bf16[384,768]{1,0:T(8,128)(2,1)S(1)} %copy-done.1, ...), custom_call_target="tpu_custom_call" | custom-call | flops 754974720 | bytes 5000000 | tf_op jit(solution)/shard_map/pallas_call | solution.py:83
  46.6 3.5 %all-to-all-start.1 = ((bf16[4,80,768]{2,1,0:T(8,128)(2,1)}), bf16[4,80,768]{2,1,0:T(8,128)(2,1)S(1)}, u32[]{:S(2)}, u32[]{:S(2)}) async-start(bf16[4,80,768]{2,1,0:T(8,128)(2,1)} %bitcast.4), calls=%async_computation.1 | async-start | bytes 983040 | tf_op jit(solution)/shard_map/all_to_all | solution.py:131
  50.0 4.8 %collective-permute-start.2 = (bf16[640,768]{1,0:T(8,128)(2,1)S(1)}, bf16[640,768]{1,0:T(8,128)(2,1)S(1)}, u32[]{:S(2)}, u32[]{:S(2)}) collective-permute-start(bf16[640,768]{1,0:T(8,128)(2,1)S(1)} %bitcast.25), channel_id=1, source_target_pairs={{0,4},{4,0},{1,5},{5,1},{2,6},{6,2},{3,7},{7,3},{8,12},{12,8},{9,1... | collective-permute-start | bytes 2949128 | tf_op jit(solution)/shard_map/ppermute | solution.py:95
  54.9 0.0 copy-done.2
  54.9 2.6 %shard_map.76 = bf16[320,768]{1,0:T(8,128)(2,1)} custom-call(s32[2]{0:T(128)S(1)} %get-tuple-element.27.place, bf16[4,2,80,768]{3,2,1,0:T(8,128)(2,1)S(1)} %bitcast.26, bf16[768,384]{1,0:T(8,128)(2,1)S(1)} %copy-done, bf16[768,384]{1,0:T(8,128)(2,1)S(1)} %collective-permute-done.got_in, bf16[384,768]{1,0:T(8,128)(2,1)S(1)} %copy-done.1, ...), custom_call_target="tpu_custom_call" | custom-call | flops 754974720 | bytes 5000000 | tf_op jit(solution)/shard_map/pallas_call | solution.py:83
  57.5 0.0 collective-permute-done.2.y
  57.5 0.9 copy-done.4
  58.4 2.1 %all-to-all-done.1 = bf16[4,80,768]{2,1,0:T(8,128)(2,1)S(1)} async-done(((bf16[4,80,768]{2,1,0:T(8,128)(2,1)}), bf16[4,80,768]{2,1,0:T(8,128)(2,1)S(1)}, u32[]{:S(2)}, u32[]{:S(2)}) %all-to-all-start.1) | async-done | bytes 491552 | tf_op jit(solution)/shard_map/all_to_all | solution.py:131
  60.5 5.2 %all-to-all-start.2 = ((bf16[4,80,768]{2,1,0:T(8,128)(2,1)}), bf16[4,80,768]{2,1,0:T(8,128)(2,1)S(1)}, u32[]{:S(2)}, u32[]{:S(2)}) async-start(bf16[4,80,768]{2,1,0:T(8,128)(2,1)} %bitcast.6), calls=%async_computation.2 | async-start | bytes 983040 | tf_op jit(solution)/shard_map/all_to_all | solution.py:131
  65.8 0.1 reduce_sum.34
  65.9 7.3 %collective-permute-start.3 = (bf16[80,768]{1,0:T(8,128)(2,1)S(1)}, bf16[80,768]{1,0:T(8,128)(2,1)S(1)}, u32[]{:S(2)}, u32[]{:S(2)}) collective-permute-start(bf16[80,768]{1,0:T(8,128)(2,1)S(1)} %reduce_sum.34), channel_id=1, source_target_pairs={{0,256},{256,0},{1,257},{257,1},{2,258},{258,2},{3,259},{259,3},{4... | collective-permute-start | bytes 368648 | tf_op jit(solution)/shard_map/ppermute | solution.py:95
  73.2 7.6 %all-to-all-done.2 = bf16[4,80,768]{2,1,0:T(8,128)(2,1)S(1)} async-done(((bf16[4,80,768]{2,1,0:T(8,128)(2,1)}), bf16[4,80,768]{2,1,0:T(8,128)(2,1)S(1)}, u32[]{:S(2)}, u32[]{:S(2)}) %all-to-all-start.2) | async-done | bytes 491552 | tf_op jit(solution)/shard_map/all_to_all | solution.py:131
  80.8 0.1 convert_reduce_fusion
  80.8 0.0 collective-permute-done.3
  80.9 6.6 %all-gather = bf16[160,768]{1,0:T(8,128)(2,1)S(1)} all-gather(bf16[80,768]{1,0:T(8,128)(2,1)S(1)} %fusion.14), channel_id=2, replica_groups=mesh['za'=2,'zb'=2,'zc'=2,'zhi'=2,'x'=4,'core'=2,'y'=4] {'core'}, dimensions={0}, use_global_device_ids=true | all-gather | bytes 368640 | tf_op jit(solution)/shard_map/all_gather | solution.py:139
  87.5 0.3 fusion.5
  87.8 17.0 %all_gather.24 = bf16[160,768]{1,0:T(8,128)(2,1)S(1)} all-gather(bf16[80,768]{1,0:T(8,128)(2,1)S(1)} %fusion.5), channel_id=1, replica_groups=mesh['za'=2,'zb'=2,'zc'=2,'zhi'=2,'x'=4,'core'=2,'y'=4] {'za'}, dimensions={0}, use_global_device_ids=true | all-gather | bytes 368640 | tf_op jit(solution)/shard_map/all_gather | solution.py:141
  104.8 18.3 %all_gather.25.g = bf16[640,768]{1,0:T(8,128)(2,1)S(1)} all-gather(bf16[160,768]{1,0:T(8,128)(2,1)S(1)} %all_gather.24), channel_id=1, replica_groups=mesh['za'=2,'zb'=2,'zc'=2,'zhi'=2,'x'=4,'core'=2,'y'=4] {'zb','zc'}, dimensions={0}, use_global_device_ids=true | all-gather | bytes 1228800 | tf_op jit(solution)/shard_map/all_gather | solution.py:142
  123.1 0.0 copy-done.3
  123.1 2.3 %shard_map.77 = (bf16[640,768]{1,0:T(8,128)(2,1)S(1)}, bf16[640,384]{1,0:T(8,128)(2,1)S(1)}) custom-call(s32[1]{0:T(128)} %bitcast.core, bf16[640,768]{1,0:T(8,128)(2,1)S(1)} %all_gather.25.g, bf16[768,384]{1,0:T(8,128)(2,1)S(1)} %copy-done, bf16[768,384]{1,0:T(8,128)(2,1)S(1)} %copy-done.3, bf16[384,768]{1,0:T(8,128)(2,1)S(1)} %copy-done.1, ...), custom_call_target="tpu_custom_call" | custom-call | flops 754974720 | bytes 5000000 | tf_op jit(solution)/shard_map/pallas_call | solution.py:83
  125.3 0.0 copy-start.6
  125.3 1.0 copy-done.6
  126.3 0.8 copy-done.7
  127.1 7.1 %all-to-all-start.3 = ((bf16[16,40,768]{2,1,0:T(8,128)(2,1)}), bf16[16,40,768]{2,1,0:T(8,128)(2,1)}, u32[]{:S(2)}, u32[]{:S(2)}) async-start(bf16[16,40,768]{2,1,0:T(8,128)(2,1)} %bitcast.28), calls=%async_computation.3 | async-start | bytes 1966080 | tf_op jit(solution)/shard_map/all_to_all | solution.py:146
  134.2 3.8 %collective-permute-start.4 = (bf16[640,384]{1,0:T(8,128)(2,1)}, bf16[640,384]{1,0:T(8,128)(2,1)}, u32[]{:S(2)}, u32[]{:S(2)}) collective-permute-start(bf16[640,384]{1,0:T(8,128)(2,1)} %copy-done.7), channel_id=1, source_target_pairs={{0,4},{4,0},{1,5},{5,1},{2,6},{6,2},{3,7},{7,3},{8,12},{12,8},{9,1... | collective-permute-start | bytes 1474568 | tf_op jit(solution)/shard_map/ppermute | solution.py:95
  138.0 1.8 %collective-permute-done.4.k = bf16[640,384]{1,0:T(8,128)(2,1)} collective-permute-done((bf16[640,384]{1,0:T(8,128)(2,1)}, bf16[640,384]{1,0:T(8,128)(2,1)}, u32[]{:S(2)}, u32[]{:S(2)}) %collective-permute-start.4) | collective-permute-done | bytes 491552 | tf_op jit(solution)/shard_map/ppermute | solution.py:95
  139.8 0.0 copy-done.5
  139.8 3.7 %shard_map.78 = (f32[768,384]{1,0:T(8,128)}, f32[384,768]{1,0:T(8,128)}) custom-call(s32[1]{0:T(128)} %bitcast.core, bf16[640,768]{1,0:T(8,128)(2,1)S(1)} %bitcast.27, bf16[640,768]{1,0:T(8,128)(2,1)S(1)} %copy-done.5, bf16[640,768]{1,0:T(8,128)(2,1)S(1)} %all_gather.25.g, bf16[640,384]{1,0:T(8,128)(2,1)} %collective-permute-done.4.k), custom_call_target="tpu_custom_call" | custom-call | flops 754974720 | bytes 5000000 | tf_op jit(solution)/shard_map/pallas_call | solution.py:83
  143.5 5.1 %all-to-all-done.3 = bf16[16,40,768]{2,1,0:T(8,128)(2,1)} async-done(((bf16[16,40,768]{2,1,0:T(8,128)(2,1)}), bf16[16,40,768]{2,1,0:T(8,128)(2,1)}, u32[]{:S(2)}, u32[]{:S(2)}) %all-to-all-start.3) | async-done | bytes 983072 | tf_op jit(solution)/shard_map/all_to_all | solution.py:146
  148.6 1.4 reduce_sum.35
  150.0 17.5 %all-gather.1 = bf16[160,768]{1,0:T(8,128)(2,1)S(1)} all-gather(bf16[40,768]{1,0:T(8,128)(2,1)S(1)} %reduce_sum.35), channel_id=3, replica_groups=mesh['za'=2,'zb'=2,'zc'=2,'zhi'=2,'x'=4,'core'=2,'y'=4] {'zhi','core'}, dimensions={0}, use_global_device_ids=true | all-gather | bytes 307200 | tf_op jit(solution)/shard_map/all_gather | solution.py:151
  167.4 0.1 reshape.43
  167.6 0.0 copy-done.8
  167.6 0.0 copy-done.9
  167.6 0.6 fusion.17
  (13 shorter events, 0.1 us)
Async XLA Ops:
  23.5 5.2 %copy-start = (bf16[768,384]{1,0:T(8,128)(2,1)S(1)}, bf16[768,384]{1,0:T(8,128)(2,1)}, u32[]{:S(2)}) copy-start(bf16[768,384]{1,0:T(8,128)(2,1)} %own_in.5) | copy-start | bytes 1769476
  23.5 7.6 %copy-start.1 = (bf16[384,768]{1,0:T(8,128)(2,1)S(1)}, bf16[384,768]{1,0:T(8,128)(2,1)}, u32[]{:S(2)}) copy-start(bf16[384,768]{1,0:T(8,128)(2,1)} %own_out.5) | copy-start | bytes 1769476
  23.5 20.4 %all-to-all-start = ((bf16[16,40,768]{2,1,0:T(8,128)(2,1)}), bf16[16,40,768]{2,1,0:T(8,128)(2,1)S(1)}, u32[]{:S(2)}, u32[]{:S(2)}) async-start(bf16[16,40,768]{2,1,0:T(8,128)(2,1)} %broadcast_in_dim.2), calls=%async_computation | async-start | bytes 1966080 | tf_op jit(solution)/shard_map/all_to_all | solution.py:116
  28.7 4.4 %collective-permute-start = (bf16[768,384]{1,0:T(8,128)(2,1)S(1)}, bf16[768,384]{1,0:T(8,128)(2,1)S(1)}, u32[]{:S(2)}, u32[]{:S(2)}) collective-permute-start(bf16[768,384]{1,0:T(8,128)(2,1)S(1)} %copy-done), channel_id=1, source_target_pairs={{0,4},{4,0},{1,5},{5,1},{2,6},{6,2},{3,7},{7,3},{8,12},{12,8},{9,1... | collective-permute-start | bytes 1769480 | tf_op jit(solution)/shard_map/ppermute | solution.py:95
  31.1 4.0 %collective-permute-start.1 = (bf16[384,768]{1,0:T(8,128)(2,1)S(1)}, bf16[384,768]{1,0:T(8,128)(2,1)}, u32[]{:S(2)}, u32[]{:S(2)}) collective-permute-start(bf16[384,768]{1,0:T(8,128)(2,1)S(1)} %copy-done.1), channel_id=1, source_target_pairs={{0,4},{4,0},{1,5},{5,1},{2,6},{6,2},{3,7},{7,3},{8,12},{12,8},{9,1... | collective-permute-start | bytes 1769480 | tf_op jit(solution)/shard_map/ppermute | solution.py:95
  33.2 21.7 %copy-start.2 = (bf16[768,384]{1,0:T(8,128)(2,1)}, bf16[768,384]{1,0:T(8,128)(2,1)S(1)}, u32[]{:S(2)}) copy-start(bf16[768,384]{1,0:T(8,128)(2,1)S(1)} %collective-permute-done.got_in) | copy-start | bytes 1769476
  46.6 14.0 %all-to-all-start.1 = ((bf16[4,80,768]{2,1,0:T(8,128)(2,1)}), bf16[4,80,768]{2,1,0:T(8,128)(2,1)S(1)}, u32[]{:S(2)}, u32[]{:S(2)}) async-start(bf16[4,80,768]{2,1,0:T(8,128)(2,1)} %bitcast.4), calls=%async_computation.1 | async-start | bytes 983040 | tf_op jit(solution)/shard_map/all_to_all | solution.py:131
  50.0 7.4 %collective-permute-start.2 = (bf16[640,768]{1,0:T(8,128)(2,1)S(1)}, bf16[640,768]{1,0:T(8,128)(2,1)S(1)}, u32[]{:S(2)}, u32[]{:S(2)}) collective-permute-start(bf16[640,768]{1,0:T(8,128)(2,1)S(1)} %bitcast.25), channel_id=1, source_target_pairs={{0,4},{4,0},{1,5},{5,1},{2,6},{6,2},{3,7},{7,3},{8,12},{12,8},{9,1... | collective-permute-start | bytes 2949128 | tf_op jit(solution)/shard_map/ppermute | solution.py:95
  57.5 0.9 copy-start.4
  60.5 20.2 %all-to-all-start.2 = ((bf16[4,80,768]{2,1,0:T(8,128)(2,1)}), bf16[4,80,768]{2,1,0:T(8,128)(2,1)S(1)}, u32[]{:S(2)}, u32[]{:S(2)}) async-start(bf16[4,80,768]{2,1,0:T(8,128)(2,1)} %bitcast.6), calls=%async_computation.2 | async-start | bytes 983040 | tf_op jit(solution)/shard_map/all_to_all | solution.py:131
  65.9 15.0 %collective-permute-start.3 = (bf16[80,768]{1,0:T(8,128)(2,1)S(1)}, bf16[80,768]{1,0:T(8,128)(2,1)S(1)}, u32[]{:S(2)}, u32[]{:S(2)}) collective-permute-start(bf16[80,768]{1,0:T(8,128)(2,1)S(1)} %reduce_sum.34), channel_id=1, source_target_pairs={{0,256},{256,0},{1,257},{257,1},{2,258},{258,2},{3,259},{259,3},{4... | collective-permute-start | bytes 368648 | tf_op jit(solution)/shard_map/ppermute | solution.py:95
  87.5 35.6 %copy-start.3 = (bf16[768,384]{1,0:T(8,128)(2,1)S(1)}, bf16[768,384]{1,0:T(8,128)(2,1)}, u32[]{:S(2)}) copy-start(bf16[768,384]{1,0:T(8,128)(2,1)} %copy-done.2) | copy-start | bytes 1769476
  125.3 1.0 copy-start.6
  126.3 0.8 copy-start.7
  127.1 12.7 %copy-start.5 = (bf16[640,768]{1,0:T(8,128)(2,1)S(1)}, bf16[640,768]{1,0:T(8,128)(2,1)}, u32[]{:S(2)}) copy-start(bf16[640,768]{1,0:T(8,128)(2,1)} %copy-done.4) | copy-start | bytes 2949124
  127.1 21.5 %all-to-all-start.3 = ((bf16[16,40,768]{2,1,0:T(8,128)(2,1)}), bf16[16,40,768]{2,1,0:T(8,128)(2,1)}, u32[]{:S(2)}, u32[]{:S(2)}) async-start(bf16[16,40,768]{2,1,0:T(8,128)(2,1)} %bitcast.28), calls=%async_computation.3 | async-start | bytes 1966080 | tf_op jit(solution)/shard_map/all_to_all | solution.py:146
  134.2 5.6 %collective-permute-start.4 = (bf16[640,384]{1,0:T(8,128)(2,1)}, bf16[640,384]{1,0:T(8,128)(2,1)}, u32[]{:S(2)}, u32[]{:S(2)}) collective-permute-start(bf16[640,384]{1,0:T(8,128)(2,1)} %copy-done.7), channel_id=1, source_target_pairs={{0,4},{4,0},{1,5},{5,1},{2,6},{6,2},{3,7},{7,3},{8,12},{12,8},{9,1... | collective-permute-start | bytes 1474568 | tf_op jit(solution)/shard_map/ppermute | solution.py:95
  148.6 19.0 %copy-start.8 = (bf16[10,768]{1,0:T(8,128)(2,1)S(1)}, bf16[10,768]{1,0:T(8,128)(2,1)}, u32[]{:S(2)}) copy-start(bf16[10,768]{1,0:T(8,128)(2,1)} %param.7) | copy-start | bytes 46084
  148.6 19.0 %copy-start.9 = (bf16[10,768]{1,0:T(8,128)(2,1)S(1)}, bf16[10,768]{1,0:T(8,128)(2,1)}, u32[]{:S(2)}) copy-start(bf16[10,768]{1,0:T(8,128)(2,1)} %param.4) | copy-start | bytes 46084

commit v4 on v3

--- a/solution.py
+++ b/solution.py
@@ -1,3 +1,5 @@
+import functools
+
 import jax
 import jax.numpy as jnp
 from jax import lax
@@ -12,6 +14,7 @@
 XY = ("x", "y")
 CHIPS = ("zhi", "core")
 SWAP = [(0, 1), (1, 0)]
+CUTS = (0, 6, 10)
 F32 = jnp.float32
 BF16 = jnp.bfloat16
 NT = (((1,), (1,)), ((), ()))
@@ -33,11 +36,11 @@
     return lax.dot_general(left, right, dims, preferred_element_type=F32)
 
 
-def first_kernel(place, x, own_in, got_in, own_out, got_out, out, rows):
+def first_kernel(low, high, place, x, own_in, got_in, own_out, got_out, out, rows):
     width = own_in.shape[1]
-    size = x.shape[2]
+    size = high - low
     for q in range(x.shape[0]):
-        rows[size * q : size * (q + 1), :] = x[q, place[1]]
+        rows[size * q : size * (q + 1), :] = x[q, low:high]
 
     @pl.when(place[0] == 0)
     def _():
@@ -50,18 +53,16 @@
         out[:, width:] = dot(rows[...], own_out[...], NT).astype(BF16)
 
 
-def second_kernel(core, g, own_in, got_in, own_out, got_out, out, give):
+def second_kernel(core, g, own_in, got_in, own_out, got_out, out):
     width = own_in.shape[1]
 
     @pl.when(core[0] == 0)
     def _():
         out[...] = (dot(g[:, :width], own_out[...]) + dot(g[:, width:], got_out[...])).astype(BF16)
-        give[...] = g[:, width:]
 
     @pl.when(core[0] == 1)
     def _():
         out[...] = (dot(g[:, :width], got_in[...], NT) + dot(g[:, width:], own_in[...], NT)).astype(BF16)
-        give[...] = g[:, :width]
 
 
 def grads_kernel(core, x, y, g, k, in_grad, out_grad):
@@ -102,12 +103,12 @@
 def body(tokens, in_weight, out_weight, cotangent):
     kept, feats = tokens.shape
     width = in_weight.shape[1]
-    core, zhi, za = lax.axis_index("core"), lax.axis_index("zhi"), lax.axis_index("za")
+    core, zhi = lax.axis_index("core"), lax.axis_index("zhi")
     is_first = core == 0
     place = core.astype(jnp.int32).reshape(1)
     spread, four = 16, 4 * kept
     count = spread * four
-    half, eighth = count // 2, count // 8
+    quarter = count // 4
     struct = jax.ShapeDtypeStruct
 
     both = lax.all_gather(jnp.concatenate([tokens, cotangent], axis=1), CHIPS, tiled=True)
@@ -116,16 +117,17 @@
     x = lax.all_to_all(block, XY, 0, 0, tiled=True).reshape(count, feats)
     weights = (in_weight, swap(in_weight, "core"), out_weight, swap(out_weight, "core"))
 
-    def terms(which):
+    def terms(low, high):
+        size = 4 * (high - low)
         out = call(
-            first_kernel,
-            struct((half, 2 * width), BF16),
-            jnp.stack([core, which]).astype(jnp.int32),
-            x.reshape(4, 2, eighth, feats),
+            functools.partial(first_kernel, low, high),
+            struct((size, 2 * width), BF16),
+            place,
+            x.reshape(4, quarter, feats),
             *weights,
-            scratch=[pltpu.VMEM((half, feats), BF16)],
+            scratch=[pltpu.VMEM((size, feats), BF16)],
         )
-        return out.reshape(4, eighth, 2 * width)
+        return out.reshape(4, high - low, 2 * width)
 
     def exchange(blocks):
         return lax.all_to_all(blocks, QUAD, 0, 0, tiled=True)
@@ -133,18 +135,30 @@
     def total(parts):
         return jnp.sum(parts.astype(F32), axis=0)
 
-    far, near, y = tie(exchange(terms(1 - za)), terms(za), swap(x, "core"))
-    came = swap(total(far).astype(BF16), "za")
-    full = total(exchange(near)) + came.astype(F32)
-    hidden = lax.all_gather(full.astype(BF16), "core")[0].astype(F32)
-    shard = jnp.where(is_first, gelu_value(full), full * gelu_slope(hidden)).astype(BF16)
-    shard = lax.all_gather(shard, "za", tiled=True)
+    def finish(near, came):
+        full = near + came.astype(F32)
+        hidden = lax.all_gather(full.astype(BF16), "core")[0].astype(F32)
+        return jnp.where(is_first, gelu_value(full), full * gelu_slope(hidden)).astype(BF16)
+
+    cuts = [quarter * tenths // 10 for tenths in CUTS]
+    nears, cames, sent = [], [], None
+    for low, high in zip(cuts[:-1], cuts[1:]):
+        part = terms(low, high)
+        if sent is not None:
+            sent, part = tie(sent, part)
+            nears.append(total(sent))
+            cames.append(swap(nears[-1].astype(BF16), "za"))
+        sent = exchange(part)
+        if low == 0:
+            sent, y = tie(sent, swap(x, "core"))
+    nears.append(total(sent))
+    cames.append(swap(nears[-1].astype(BF16), "za"))
+    shard = finish(jnp.concatenate(nears, axis=0), jnp.concatenate(cames, axis=0))
     g = lax.all_gather(shard, QUAD, tiled=True)
 
-    shapes = (struct((count, feats), BF16), struct((count, width), BF16))
-    out, give = call(second_kernel, shapes, place, g, *weights)
+    out = call(second_kernel, struct((count, feats), BF16), place, g, *weights)
     parts = lax.all_to_all(out.reshape(spread, four, feats), XY, 0, 0, tiled=True)
-    k = swap(give, "core")
+    k = swap(jnp.where(is_first, g[:, width:], g[:, :width]), "core")
     shapes = (struct((feats, width), F32), struct((width, feats), F32))
     in_grad, out_grad = call(grads_kernel, shapes, place, x, y, g, k)
     parts, in_grad, out_grad = tie(parts, in_grad, out_grad)

time: 169 us -> 167 us (0.988)
  blocking collectives: 80.4 us -> 68.4 us
  starting transfers between devices: 41.3 us -> 49.3 us
  Pallas kernels: 11.1 us -> 7.86 us
  local copies, waits for them, and re-layouts: 3.86 us -> 6.02 us
  other arithmetic: 3.31 us -> 5.38 us
    all_gather x2 -> x1, blocking collectives: 23.6 us -> 10.7 us  [finish(): hidden = lax.all_gather(full.astype(BF16), 'core')[0].astype(F32)]
    ppermute x5 -> x6, starting transfers between devices: 20.3 us -> 29.8 us  [swap(): return lax.ppermute(x, axis, SWAP)]
    ppermute x5 -> x6, waiting for transfers between devices: 3.77 us -> 8.57 us  [swap(): return lax.ppermute(x, axis, SWAP)]
    pallas_call x4, Pallas kernels: 11.1 us -> 7.86 us  [call(): pl.pallas_call(kernel, out_shape=outs, in_specs=[pl.BlockSpec(memory_spac...]
    all_to_all x2, waiting for transfers between devices: 9.72 us -> 7.01 us  [exchange(): return lax.all_to_all(blocks, QUAD, 0, 0, tiled=True)]
    unnamed x21 -> x27, local copies, waits for them, and re-layouts: 2.77 us -> 4.93 us
  transfers between devices with their start and end apart: 9 -> 10, of which waited for: 6 -> 7; matrix products, arithmetic and copies ran while one was open for 0% -> 1% of each run, Pallas kernels for 4% -> 3%
where the time goes in v4:
time: 167 us; the launch traced here: 166 us
  blocking collectives  68.4 us (41%)
  starting transfers between devices  49.3 us (30%)
  waiting for transfers between devices  28.1 us (17%)
  Pallas kernels  7.86 us (5%)
  local copies, waits for them, and re-layouts  6.02 us (4%)
  other arithmetic  5.38 us (3%)
    ppermute x6, starting transfers between devices, swap(): return lax.ppermute(x, axis, SWAP)  29.8 us
    all_gather x1, blocking collectives, body(): lax.all_gather(jnp.concatenate([tokens, cotangent], axis=1), CHIPS, tiled...  21 us
    all_gather x1, blocking collectives, body(): g = lax.all_gather(shard, QUAD, tiled=True)  19.5 us
    all_gather x1, blocking collectives, body(): lax.all_gather(total(parts).astype(BF16), CHIPS)  17.3 us
    all_gather x1, blocking collectives, finish(): hidden = lax.all_gather(full.astype(BF16), 'core')[0].astype(F32)  10.7 us
    ppermute x6, waiting for transfers between devices, swap(): return lax.ppermute(x, axis, SWAP)  8.57 us
    all_to_all x1, waiting for transfers between devices, body(): x = lax.all_to_all(block, XY, 0, 0, tiled=True).reshape(count, feats)  8.12 us
    pallas_call x4, Pallas kernels, call(): pl.pallas_call(kernel, out_shape=outs, in_specs=[pl.BlockSpec(memory_spac...  7.86 us
  transfers between devices with their start and end apart: 10, of which 7 were waited for; matrix products, arithmetic and copies ran while one was open for 1% of the time, Pallas kernels for 3%

profile of v4, /device:TPU:1, one launch (start us, length us, event | category | flops | bytes accessed | tf_op | source)
XLA Modules:
  0.0 166.0 jit_solution(2224157699571313959)
XLA Ops:
  0.6 0.8 maximum_bitcast_fusion
  1.4 21.0 %all-gather.1 = bf16[4,10,1536]{2,1,0:T(8,128)(2,1)S(1)} all-gather(bf16[1,10,1536]{2,1,0:T(8,128)(2,1)S(1)} %maximum_bitcast_fusion), channel_id=1, replica_groups=mesh['za'=2,'zb'=2,'zc'=2,'zhi'=2,'x'=4,'core'=2,'y'=4] {'zhi','core'}, dimensions={0}, use_global_device_ids=true | all-gather | bytes 153600 | tf_op jit(solution)/shard_map/all_gather | solution.py:114
  22.5 1.0 broadcast_in_dim.2
  23.5 5.2 %all-to-all-start = ((bf16[16,40,768]{2,1,0:T(8,128)(2,1)}), bf16[16,40,768]{2,1,0:T(8,128)(2,1)S(1)}, u32[]{:S(2)}, u32[]{:S(2)}) async-start(bf16[16,40,768]{2,1,0:T(8,128)(2,1)} %broadcast_in_dim.2), calls=%async_computation | async-start | bytes 1966080 | tf_op jit(solution)/shard_map/all_to_all | solution.py:117
  28.7 0.0 copy-done
  28.7 2.4 %collective-permute-start = (bf16[768,384]{1,0:T(8,128)(2,1)S(1)}, bf16[768,384]{1,0:T(8,128)(2,1)S(1)}, u32[]{:S(2)}, u32[]{:S(2)}) collective-permute-start(bf16[768,384]{1,0:T(8,128)(2,1)S(1)} %copy-done), channel_id=1, source_target_pairs={{0,4},{4,0},{1,5},{5,1},{2,6},{6,2},{3,7},{7,3},{8,12},{12,8},{9,1... | collective-permute-start | bytes 1769480 | tf_op jit(solution)/shard_map/ppermute | solution.py:96
  31.1 0.0 copy-done.1
  31.1 2.0 %collective-permute-start.1 = (bf16[384,768]{1,0:T(8,128)(2,1)S(1)}, bf16[384,768]{1,0:T(8,128)(2,1)S(1)}, u32[]{:S(2)}, u32[]{:S(2)}) collective-permute-start(bf16[384,768]{1,0:T(8,128)(2,1)S(1)} %copy-done.1), channel_id=1, source_target_pairs={{0,4},{4,0},{1,5},{5,1},{2,6},{6,2},{3,7},{7,3},{8,12},{12,8},{9,1... | collective-permute-start | bytes 1769480 | tf_op jit(solution)/shard_map/ppermute | solution.py:96
  33.1 0.0 collective-permute-done.got_in
  33.1 0.0 copy-start.2
  33.1 1.9 %collective-permute-done.1.got_out = bf16[384,768]{1,0:T(8,128)(2,1)S(1)} collective-permute-done((bf16[384,768]{1,0:T(8,128)(2,1)S(1)}, bf16[384,768]{1,0:T(8,128)(2,1)S(1)}, u32[]{:S(2)}, u32[]{:S(2)}) %collective-permute-start.1) | collective-permute-done | bytes 589856 | tf_op jit(solution)/shard_map/ppermute | solution.py:96
  35.0 0.8 copy-done.4
  35.8 8.1 %all-to-all-done = bf16[16,40,768]{2,1,0:T(8,128)(2,1)S(1)} async-done(((bf16[16,40,768]{2,1,0:T(8,128)(2,1)}), bf16[16,40,768]{2,1,0:T(8,128)(2,1)S(1)}, u32[]{:S(2)}, u32[]{:S(2)}) %all-to-all-start) | async-done | bytes 983072 | tf_op jit(solution)/shard_map/all_to_all | solution.py:117
  44.0 1.1 copy-done.5
  45.0 1.7 %shard_map.75 = bf16[384,768]{1,0:T(8,128)(2,1)} custom-call(s32[1]{0:T(128)} %bitcast.place.core, bf16[4,160,768]{2,1,0:T(8,128)(2,1)S(1)} %bitcast.31, bf16[768,384]{1,0:T(8,128)(2,1)S(1)} %copy-done, bf16[768,384]{1,0:T(8,128)(2,1)S(1)} %collective-permute-done.got_in, bf16[384,768]{1,0:T(8,128)(2,1)S(1)} %copy-done.1, bf16[384,768]{1,0:T(8,128)(2,1)S(1)} %copy-done.5), custom_call_target="tpu_custom_call" | custom-call | flops 754974720 | bytes 5000000 | tf_op jit(solution)/shard_map/pallas_call | solution.py:84
  46.7 3.5 %all-to-all-start.1 = ((bf16[4,96,768]{2,1,0:T(8,128)(2,1)}), bf16[4,96,768]{2,1,0:T(8,128)(2,1)S(1)}, u32[]{:S(2)}, u32[]{:S(2)}) async-start(bf16[4,96,768]{2,1,0:T(8,128)(2,1)} %bitcast.3), calls=%async_computation.1 | async-start | bytes 1179648 | tf_op jit(solution)/shard_map/all_to_all | solution.py:133
  50.2 4.8 %collective-permute-start.2 = (bf16[640,768]{1,0:T(8,128)(2,1)S(1)}, bf16[640,768]{1,0:T(8,128)(2,1)S(1)}, u32[]{:S(2)}, u32[]{:S(2)}) collective-permute-start(bf16[640,768]{1,0:T(8,128)(2,1)S(1)} %bitcast.32), channel_id=1, source_target_pairs={{0,4},{4,0},{1,5},{5,1},{2,6},{6,2},{3,7},{7,3},{8,12},{12,8},{9,1... | collective-permute-start | bytes 2949128 | tf_op jit(solution)/shard_map/ppermute | solution.py:96
  55.0 0.0 copy-start.6
  55.0 1.1 copy-done.6
  56.1 1.3 shard_map.76
  57.4 0.0 collective-permute-done.2.y
  57.4 0.9 copy-done.9
  58.4 6.0 %all-to-all-done.1 = bf16[4,96,768]{2,1,0:T(8,128)(2,1)S(1)} async-done(((bf16[4,96,768]{2,1,0:T(8,128)(2,1)}), bf16[4,96,768]{2,1,0:T(8,128)(2,1)S(1)}, u32[]{:S(2)}, u32[]{:S(2)}) %all-to-all-start.1) | async-done | bytes 589856 | tf_op jit(solution)/shard_map/all_to_all | solution.py:133
  64.4 4.1 %all-to-all-start.2 = ((bf16[4,64,768]{2,1,0:T(8,128)(2,1)}), bf16[4,64,768]{2,1,0:T(8,128)(2,1)}, u32[]{:S(2)}, u32[]{:S(2)}) async-start(bf16[4,64,768]{2,1,0:T(8,128)(2,1)} %bitcast.5), calls=%async_computation.2 | async-start | bytes 786432 | tf_op jit(solution)/shard_map/all_to_all | solution.py:133
  68.5 0.1 convert_reduce_fusion
  68.6 7.9 %collective-permute-start.3 = (bf16[96,768]{1,0:T(8,128)(2,1)S(1)}, bf16[96,768]{1,0:T(8,128)(2,1)S(1)}, u32[]{:S(2)}, u32[]{:S(2)}) collective-permute-start(bf16[96,768]{1,0:T(8,128)(2,1)S(1)} %convert_element_type.64), channel_id=1, source_target_pairs={{0,256},{256,0},{1,257},{257,1},{2,258},{258,2},{3,259},{259,3},{4... | collective-permute-start | bytes 442376 | tf_op jit(solution)/shard_map/ppermute | solution.py:96
  76.6 1.0 all-to-all-done.2
  77.6 1.1 convert_reduce_fusion.1
  78.7 9.0 %collective-permute-start.4 = (bf16[64,768]{1,0:T(8,128)(2,1)S(1)}, bf16[64,768]{1,0:T(8,128)(2,1)S(1)}, u32[]{:S(2)}, u32[]{:S(2)}) collective-permute-start(bf16[64,768]{1,0:T(8,128)(2,1)S(1)} %convert_element_type.65), channel_id=1, source_target_pairs={{0,256},{256,0},{1,257},{257,1},{2,258},{258,2},{3,259},{259,3},{4... | collective-permute-start | bytes 294920 | tf_op jit(solution)/shard_map/ppermute | solution.py:96
  87.7 0.0 collective-permute-done.3
  87.7 4.9 %collective-permute-done.4 = bf16[64,768]{1,0:T(8,128)(2,1)S(1)} collective-permute-done((bf16[64,768]{1,0:T(8,128)(2,1)S(1)}, bf16[64,768]{1,0:T(8,128)(2,1)S(1)}, u32[]{:S(2)}, u32[]{:S(2)}) %collective-permute-start.4) | collective-permute-done | bytes 98336 | tf_op jit(solution)/shard_map/ppermute | solution.py:96
  92.6 10.7 %all_gather.17 = bf16[2,160,768]{2,1,0:T(8,128)(2,1)S(1)} all-gather(bf16[1,160,768]{2,1,0:T(8,128)(2,1)S(1)} %fusion.14), channel_id=1, replica_groups=mesh['za'=2,'zb'=2,'zc'=2,'zhi'=2,'x'=4,'core'=2,'y'=4] {'core'}, dimensions={0}, use_global_device_ids=true | all-gather | bytes 737280 | tf_op jit(solution)/shard_map/all_gather | solution.py:140
  103.3 0.5 fusion.5
  103.8 19.5 %all_gather.18.g = bf16[640,768]{1,0:T(8,128)(2,1)S(1)} all-gather(bf16[160,768]{1,0:T(8,128)(2,1)S(1)} %fusion.5), channel_id=1, replica_groups=mesh['za'=2,'zb'=2,'zc'=2,'zhi'=2,'x'=4,'core'=2,'y'=4] {'zb','zc'}, dimensions={0}, use_global_device_ids=true | all-gather | bytes 1228800 | tf_op jit(solution)/shard_map/all_gather | solution.py:157
  123.3 0.0 copy-done.7
  123.3 1.2 shard_map.77
  124.5 1.0 copy-done.8
  125.5 6.7 %all-to-all-start.3 = ((bf16[16,40,768]{2,1,0:T(8,128)(2,1)}), bf16[16,40,768]{2,1,0:T(8,128)(2,1)}, u32[]{:S(2)}, u32[]{:S(2)}) async-start(bf16[16,40,768]{2,1,0:T(8,128)(2,1)} %bitcast.35), calls=%async_computation.3 | async-start | bytes 1966080 | tf_op jit(solution)/shard_map/all_to_all | solution.py:160
  132.2 0.0 copy-start.10
  132.2 0.8 slice_select_fusion
  133.0 3.7 %collective-permute-start.5 = (bf16[640,384]{1,0:T(8,128)(2,1)}, bf16[640,384]{1,0:T(8,128)(2,1)}, u32[]{:S(2)}, u32[]{:S(2)}) collective-permute-start(bf16[640,384]{1,0:T(8,128)(2,1)} %slice_select_fusion), channel_id=1, source_target_pairs={{0,4},{4,0},{1,5},{5,1},{2,6},{6,2},{3,7},{7,3},{8,12},{12,8},{9,1... | collective-permute-start | bytes 1474568 | tf_op jit(solution)/shard_map/ppermute | solution.py:96
  136.7 1.8 %collective-permute-done.5.k = bf16[640,384]{1,0:T(8,128)(2,1)} collective-permute-done((bf16[640,384]{1,0:T(8,128)(2,1)}, bf16[640,384]{1,0:T(8,128)(2,1)}, u32[]{:S(2)}, u32[]{:S(2)}) %collective-permute-start.5) | collective-permute-done | bytes 491552 | tf_op jit(solution)/shard_map/ppermute | solution.py:96
  138.5 3.7 %shard_map.78 = (f32[768,384]{1,0:T(8,128)}, f32[384,768]{1,0:T(8,128)}) custom-call(s32[1]{0:T(128)} %bitcast.place.core, bf16[640,768]{1,0:T(8,128)(2,1)S(1)} %bitcast.34, bf16[640,768]{1,0:T(8,128)(2,1)S(1)} %copy-done.10, bf16[640,768]{1,0:T(8,128)(2,1)S(1)} %all_gather.18.g, bf16[640,384]{1,0:T(8,128)(2,1)} %collective-permute-done.5.k), custom_call_target="tpu_custom_call" | custom-call | flops 754974720 | bytes 5000000 | tf_op jit(solution)/shard_map/pallas_call | solution.py:84
  142.2 4.4 %all-to-all-done.3 = bf16[16,40,768]{2,1,0:T(8,128)(2,1)} async-done(((bf16[16,40,768]{2,1,0:T(8,128)(2,1)}), bf16[16,40,768]{2,1,0:T(8,128)(2,1)}, u32[]{:S(2)}, u32[]{:S(2)}) %all-to-all-start.3) | async-done | bytes 983072 | tf_op jit(solution)/shard_map/all_to_all | solution.py:160
  146.6 1.4 reduce_sum.32
  148.0 17.3 %all-gather = bf16[160,768]{1,0:T(8,128)(2,1)S(1)} all-gather(bf16[40,768]{1,0:T(8,128)(2,1)S(1)} %reduce_sum.32), channel_id=2, replica_groups=mesh['za'=2,'zb'=2,'zc'=2,'zhi'=2,'x'=4,'core'=2,'y'=4] {'zhi','core'}, dimensions={0}, use_global_device_ids=true | all-gather | bytes 307200 | tf_op jit(solution)/shard_map/all_gather | solution.py:165
  165.2 0.1 reshape.104
  165.4 0.6 fusion.17
  (22 shorter events, 0.2 us)
Async XLA Ops:
  23.5 5.2 %copy-start = (bf16[768,384]{1,0:T(8,128)(2,1)S(1)}, bf16[768,384]{1,0:T(8,128)(2,1)}, u32[]{:S(2)}) copy-start(bf16[768,384]{1,0:T(8,128)(2,1)} %own_in.5) | copy-start | bytes 1769476
  23.5 7.6 %copy-start.1 = (bf16[384,768]{1,0:T(8,128)(2,1)S(1)}, bf16[384,768]{1,0:T(8,128)(2,1)}, u32[]{:S(2)}) copy-start(bf16[384,768]{1,0:T(8,128)(2,1)} %own_out.5) | copy-start | bytes 1769476
  23.5 20.4 %all-to-all-start = ((bf16[16,40,768]{2,1,0:T(8,128)(2,1)}), bf16[16,40,768]{2,1,0:T(8,128)(2,1)S(1)}, u32[]{:S(2)}, u32[]{:S(2)}) async-start(bf16[16,40,768]{2,1,0:T(8,128)(2,1)} %broadcast_in_dim.2), calls=%async_computation | async-start | bytes 1966080 | tf_op jit(solution)/shard_map/all_to_all | solution.py:117
  28.7 4.4 %collective-permute-start = (bf16[768,384]{1,0:T(8,128)(2,1)S(1)}, bf16[768,384]{1,0:T(8,128)(2,1)S(1)}, u32[]{:S(2)}, u32[]{:S(2)}) collective-permute-start(bf16[768,384]{1,0:T(8,128)(2,1)S(1)} %copy-done), channel_id=1, source_target_pairs={{0,4},{4,0},{1,5},{5,1},{2,6},{6,2},{3,7},{7,3},{8,12},{12,8},{9,1... | collective-permute-start | bytes 1769480 | tf_op jit(solution)/shard_map/ppermute | solution.py:96
  31.1 3.9 %collective-permute-start.1 = (bf16[384,768]{1,0:T(8,128)(2,1)S(1)}, bf16[384,768]{1,0:T(8,128)(2,1)S(1)}, u32[]{:S(2)}, u32[]{:S(2)}) collective-permute-start(bf16[384,768]{1,0:T(8,128)(2,1)S(1)} %copy-done.1), channel_id=1, source_target_pairs={{0,4},{4,0},{1,5},{5,1},{2,6},{6,2},{3,7},{7,3},{8,12},{12,8},{9,1... | collective-permute-start | bytes 1769480 | tf_op jit(solution)/shard_map/ppermute | solution.py:96
  33.1 21.9 %copy-start.2 = (bf16[768,384]{1,0:T(8,128)(2,1)}, bf16[768,384]{1,0:T(8,128)(2,1)S(1)}, u32[]{:S(2)}) copy-start(bf16[768,384]{1,0:T(8,128)(2,1)S(1)} %collective-permute-done.got_in) | copy-start | bytes 1769476
  35.0 0.8 copy-start.4
  44.0 1.1 copy-start.5
  46.7 17.7 %all-to-all-start.1 = ((bf16[4,96,768]{2,1,0:T(8,128)(2,1)}), bf16[4,96,768]{2,1,0:T(8,128)(2,1)S(1)}, u32[]{:S(2)}, u32[]{:S(2)}) async-start(bf16[4,96,768]{2,1,0:T(8,128)(2,1)} %bitcast.3), calls=%async_computation.1 | async-start | bytes 1179648 | tf_op jit(solution)/shard_map/all_to_all | solution.py:133
  50.2 7.3 %collective-permute-start.2 = (bf16[640,768]{1,0:T(8,128)(2,1)S(1)}, bf16[640,768]{1,0:T(8,128)(2,1)S(1)}, u32[]{:S(2)}, u32[]{:S(2)}) collective-permute-start(bf16[640,768]{1,0:T(8,128)(2,1)S(1)} %bitcast.32), channel_id=1, source_target_pairs={{0,4},{4,0},{1,5},{5,1},{2,6},{6,2},{3,7},{7,3},{8,12},{12,8},{9,1... | collective-permute-start | bytes 2949128 | tf_op jit(solution)/shard_map/ppermute | solution.py:96
  55.0 1.1 copy-start.6
  57.4 0.9 copy-start.9
  64.4 13.2 %all-to-all-start.2 = ((bf16[4,64,768]{2,1,0:T(8,128)(2,1)}), bf16[4,64,768]{2,1,0:T(8,128)(2,1)}, u32[]{:S(2)}, u32[]{:S(2)}) async-start(bf16[4,64,768]{2,1,0:T(8,128)(2,1)} %bitcast.5), calls=%async_computation.2 | async-start | bytes 786432 | tf_op jit(solution)/shard_map/all_to_all | solution.py:133
  68.6 19.1 %collective-permute-start.3 = (bf16[96,768]{1,0:T(8,128)(2,1)S(1)}, bf16[96,768]{1,0:T(8,128)(2,1)S(1)}, u32[]{:S(2)}, u32[]{:S(2)}) collective-permute-start(bf16[96,768]{1,0:T(8,128)(2,1)S(1)} %convert_element_type.64), channel_id=1, source_target_pairs={{0,256},{256,0},{1,257},{257,1},{2,258},{258,2},{3,259},{259,3},{4... | collective-permute-start | bytes 442376 | tf_op jit(solution)/shard_map/ppermute | solution.py:96
  78.7 13.9 %collective-permute-start.4 = (bf16[64,768]{1,0:T(8,128)(2,1)S(1)}, bf16[64,768]{1,0:T(8,128)(2,1)S(1)}, u32[]{:S(2)}, u32[]{:S(2)}) collective-permute-start(bf16[64,768]{1,0:T(8,128)(2,1)S(1)} %convert_element_type.65), channel_id=1, source_target_pairs={{0,256},{256,0},{1,257},{257,1},{2,258},{258,2},{3,259},{259,3},{4... | collective-permute-start | bytes 294920 | tf_op jit(solution)/shard_map/ppermute | solution.py:96
  103.3 20.0 %copy-start.3 = (bf16[768,384]{1,0:T(8,128)(2,1)S(1)}, bf16[768,384]{1,0:T(8,128)(2,1)}, u32[]{:S(2)}) copy-start(bf16[768,384]{1,0:T(8,128)(2,1)} %copy-done.2) | copy-start | bytes 1769476
  103.3 20.0 %copy-start.7 = (bf16[384,768]{1,0:T(8,128)(2,1)S(1)}, bf16[384,768]{1,0:T(8,128)(2,1)}, u32[]{:S(2)}) copy-start(bf16[384,768]{1,0:T(8,128)(2,1)} %copy-done.4) | copy-start | bytes 1769476
  124.5 1.0 copy-start.8
  125.5 21.2 %all-to-all-start.3 = ((bf16[16,40,768]{2,1,0:T(8,128)(2,1)}), bf16[16,40,768]{2,1,0:T(8,128)(2,1)}, u32[]{:S(2)}, u32[]{:S(2)}) async-start(bf16[16,40,768]{2,1,0:T(8,128)(2,1)} %bitcast.35), calls=%async_computation.3 | async-start | bytes 1966080 | tf_op jit(solution)/shard_map/all_to_all | solution.py:160
  132.2 6.4 %copy-start.10 = (bf16[640,768]{1,0:T(8,128)(2,1)S(1)}, bf16[640,768]{1,0:T(8,128)(2,1)}, u32[]{:S(2)}) copy-start(bf16[640,768]{1,0:T(8,128)(2,1)} %copy-done.9) | copy-start | bytes 2949124
  133.0 5.5 %collective-permute-start.5 = (bf16[640,384]{1,0:T(8,128)(2,1)}, bf16[640,384]{1,0:T(8,128)(2,1)}, u32[]{:S(2)}, u32[]{:S(2)}) collective-permute-start(bf16[640,384]{1,0:T(8,128)(2,1)} %slice_select_fusion), channel_id=1, source_target_pairs={{0,4},{4,0},{1,5},{5,1},{2,6},{6,2},{3,7},{7,3},{8,12},{12,8},{9,1... | collective-permute-start | bytes 1474568 | tf_op jit(solution)/shard_map/ppermute | solution.py:96
  146.6 18.8 %copy-start.11 = (bf16[10,768]{1,0:T(8,128)(2,1)S(1)}, bf16[10,768]{1,0:T(8,128)(2,1)}, u32[]{:S(2)}) copy-start(bf16[10,768]{1,0:T(8,128)(2,1)} %param.7) | copy-start | bytes 46084
  146.6 18.8 %copy-start.12 = (bf16[10,768]{1,0:T(8,128)(2,1)S(1)}, bf16[10,768]{1,0:T(8,128)(2,1)}, u32[]{:S(2)}) copy-start(bf16[10,768]{1,0:T(8,128)(2,1)} %param.4) | copy-start | bytes 46084

commit v5 on v4

--- a/solution.py
+++ b/solution.py
@@ -14,7 +14,7 @@
 XY = ("x", "y")
 CHIPS = ("zhi", "core")
 SWAP = [(0, 1), (1, 0)]
-CUTS = (0, 6, 10)
+CUTS = (0, 7, 10)
 F32 = jnp.float32
 BF16 = jnp.bfloat16
 NT = (((1,), (1,)), ((), ()))
@@ -152,7 +152,8 @@
         if low == 0:
             sent, y = tie(sent, swap(x, "core"))
     nears.append(total(sent))
-    cames.append(swap(nears[-1].astype(BF16), "za"))
+    both = lax.all_gather(nears[-1].astype(BF16), "za")
+    cames.append(jnp.where(lax.axis_index("za") == 0, both[1], both[0]))
     shard = finish(jnp.concatenate(nears, axis=0), jnp.concatenate(cames, axis=0))
     g = lax.all_gather(shard, QUAD, tiled=True)
 

time: 167 us -> 167 us (level)
  blocking collectives: 68.4 us -> 82.6 us
  starting transfers between devices: 49.3 us -> 38.6 us
  waiting for transfers between devices: 28.1 us -> 25 us
    all_gather x0 -> x1, blocking collectives: none -> 12.5 us  [body(): both = lax.all_gather(nears[-1].astype(BF16), 'za')]
    ppermute x6 -> x5, starting transfers between devices: 29.8 us -> 20.8 us  [swap(): return lax.ppermute(x, axis, SWAP)]
    ppermute x6 -> x5, waiting for transfers between devices: 8.57 us -> 3.71 us  [swap(): return lax.ppermute(x, axis, SWAP)]
    all_to_all x2, waiting for transfers between devices: 7.01 us -> 8.74 us  [exchange(): return lax.all_to_all(blocks, QUAD, 0, 0, tiled=True)]
  transfers between devices with their start and end apart: 10 -> 9, of which waited for: 7 -> 5; matrix products, arithmetic and copies ran while one was open for 1% -> 1% of each run, Pallas kernels for 3% -> 3%
where the time goes in v5:
time: 167 us; the launch traced here: 166 us
  blocking collectives  82.6 us (49%)
  starting transfers between devices  38.6 us (23%)
  waiting for transfers between devices  25 us (15%)
  Pallas kernels  7.91 us (5%)
  local copies, waits for them, and re-layouts  6.03 us (4%)
  other arithmetic  5.37 us (3%)
    all_gather x1, blocking collectives, body(): lax.all_gather(jnp.concatenate([tokens, cotangent], axis=1), CHIPS, tiled...  21 us
    ppermute x5, starting transfers between devices, swap(): return lax.ppermute(x, axis, SWAP)  20.8 us
    all_gather x1, blocking collectives, body(): g = lax.all_gather(shard, QUAD, tiled=True)  19.5 us
    all_gather x1, blocking collectives, body(): lax.all_gather(total(parts).astype(BF16), CHIPS)  18.2 us
    all_gather x1, blocking collectives, body(): both = lax.all_gather(nears[-1].astype(BF16), 'za')  12.5 us
    all_gather x1, blocking collectives, finish(): hidden = lax.all_gather(full.astype(BF16), 'core')[0].astype(F32)  11.4 us
    all_to_all x2, waiting for transfers between devices, exchange(): return lax.all_to_all(blocks, QUAD, 0, 0, tiled=True)  8.74 us
    all_to_all x1, waiting for transfers between devices, body(): x = lax.all_to_all(block, XY, 0, 0, tiled=True).reshape(count, feats)  8.12 us
  transfers between devices with their start and end apart: 9, of which 5 were waited for; matrix products, arithmetic and copies ran while one was open for 1% of the time, Pallas kernels for 3%

profile of v5, /device:TPU:1, one launch (start us, length us, event | category | flops | bytes accessed | tf_op | source)
XLA Modules:
  0.0 166.4 jit_solution(983288293983099601)
XLA Ops:
  0.6 0.8 maximum_bitcast_fusion
  1.4 21.0 %all-gather.1 = bf16[4,10,1536]{2,1,0:T(8,128)(2,1)S(1)} all-gather(bf16[1,10,1536]{2,1,0:T(8,128)(2,1)S(1)} %maximum_bitcast_fusion), channel_id=1, replica_groups=mesh['za'=2,'zb'=2,'zc'=2,'zhi'=2,'x'=4,'core'=2,'y'=4] {'zhi','core'}, dimensions={0}, use_global_device_ids=true | all-gather | bytes 153600 | tf_op jit(solution)/shard_map/all_gather | solution.py:114
  22.5 1.0 broadcast_in_dim.2
  23.5 5.2 %all-to-all-start = ((bf16[16,40,768]{2,1,0:T(8,128)(2,1)}), bf16[16,40,768]{2,1,0:T(8,128)(2,1)S(1)}, u32[]{:S(2)}, u32[]{:S(2)}) async-start(bf16[16,40,768]{2,1,0:T(8,128)(2,1)} %broadcast_in_dim.2), calls=%async_computation | async-start | bytes 1966080 | tf_op jit(solution)/shard_map/all_to_all | solution.py:117
  28.7 0.0 copy-done
  28.7 2.4 %collective-permute-start = (bf16[768,384]{1,0:T(8,128)(2,1)S(1)}, bf16[768,384]{1,0:T(8,128)(2,1)S(1)}, u32[]{:S(2)}, u32[]{:S(2)}) collective-permute-start(bf16[768,384]{1,0:T(8,128)(2,1)S(1)} %copy-done), channel_id=1, source_target_pairs={{0,4},{4,0},{1,5},{5,1},{2,6},{6,2},{3,7},{7,3},{8,12},{12,8},{9,1... | collective-permute-start | bytes 1769480 | tf_op jit(solution)/shard_map/ppermute | solution.py:96
  31.1 0.0 copy-done.1
  31.1 2.0 %collective-permute-start.1 = (bf16[384,768]{1,0:T(8,128)(2,1)S(1)}, bf16[384,768]{1,0:T(8,128)(2,1)S(1)}, u32[]{:S(2)}, u32[]{:S(2)}) collective-permute-start(bf16[384,768]{1,0:T(8,128)(2,1)S(1)} %copy-done.1), channel_id=1, source_target_pairs={{0,4},{4,0},{1,5},{5,1},{2,6},{6,2},{3,7},{7,3},{8,12},{12,8},{9,1... | collective-permute-start | bytes 1769480 | tf_op jit(solution)/shard_map/ppermute | solution.py:96
  33.1 0.0 collective-permute-done.got_in
  33.1 0.0 copy-start.2
  33.1 1.9 %collective-permute-done.1.got_out = bf16[384,768]{1,0:T(8,128)(2,1)S(1)} collective-permute-done((bf16[384,768]{1,0:T(8,128)(2,1)S(1)}, bf16[384,768]{1,0:T(8,128)(2,1)S(1)}, u32[]{:S(2)}, u32[]{:S(2)}) %collective-permute-start.1) | collective-permute-done | bytes 589856 | tf_op jit(solution)/shard_map/ppermute | solution.py:96
  35.0 0.8 copy-done.4
  35.8 8.1 %all-to-all-done = bf16[16,40,768]{2,1,0:T(8,128)(2,1)S(1)} async-done(((bf16[16,40,768]{2,1,0:T(8,128)(2,1)}), bf16[16,40,768]{2,1,0:T(8,128)(2,1)S(1)}, u32[]{:S(2)}, u32[]{:S(2)}) %all-to-all-start) | async-done | bytes 983072 | tf_op jit(solution)/shard_map/all_to_all | solution.py:117
  44.0 1.1 copy-done.5
  45.0 1.8 %shard_map.75 = bf16[448,768]{1,0:T(8,128)(2,1)} custom-call(s32[1]{0:T(128)} %bitcast.place.core, bf16[4,160,768]{2,1,0:T(8,128)(2,1)S(1)} %bitcast.33, bf16[768,384]{1,0:T(8,128)(2,1)S(1)} %copy-done, bf16[768,384]{1,0:T(8,128)(2,1)S(1)} %collective-permute-done.got_in, bf16[384,768]{1,0:T(8,128)(2,1)S(1)} %copy-done.1, bf16[384,768]{1,0:T(8,128)(2,1)S(1)} %copy-done.5), custom_call_target="tpu_custom_call" | custom-call | flops 754974720 | bytes 5000000 | tf_op jit(solution)/shard_map/pallas_call | solution.py:84
  46.8 3.5 %all-to-all-start.1 = ((bf16[4,112,768]{2,1,0:T(8,128)(2,1)}), bf16[4,112,768]{2,1,0:T(8,128)(2,1)S(1)}, u32[]{:S(2)}, u32[]{:S(2)}) async-start(bf16[4,112,768]{2,1,0:T(8,128)(2,1)} %bitcast.3), calls=%async_computation.1 | async-start | bytes 1376256 | tf_op jit(solution)/shard_map/all_to_all | solution.py:133
  50.3 4.8 %collective-permute-start.2 = (bf16[640,768]{1,0:T(8,128)(2,1)S(1)}, bf16[640,768]{1,0:T(8,128)(2,1)S(1)}, u32[]{:S(2)}, u32[]{:S(2)}) collective-permute-start(bf16[640,768]{1,0:T(8,128)(2,1)S(1)} %bitcast.34), channel_id=1, source_target_pairs={{0,4},{4,0},{1,5},{5,1},{2,6},{6,2},{3,7},{7,3},{8,12},{12,8},{9,1... | collective-permute-start | bytes 2949128 | tf_op jit(solution)/shard_map/ppermute | solution.py:96
  55.1 1.1 copy-done.6
  56.2 1.3 shard_map.76
  57.5 0.0 collective-permute-done.2.y
  57.5 0.9 copy-done.9
  58.4 8.7 %all-to-all-done.1 = bf16[4,112,768]{2,1,0:T(8,128)(2,1)S(1)} async-done(((bf16[4,112,768]{2,1,0:T(8,128)(2,1)}), bf16[4,112,768]{2,1,0:T(8,128)(2,1)S(1)}, u32[]{:S(2)}, u32[]{:S(2)}) %all-to-all-start.1) | async-done | bytes 688160 | tf_op jit(solution)/shard_map/all_to_all | solution.py:133
  67.2 4.1 %all-to-all-start.2 = ((bf16[4,48,768]{2,1,0:T(8,128)(2,1)}), bf16[4,48,768]{2,1,0:T(8,128)(2,1)}, u32[]{:S(2)}, u32[]{:S(2)}) async-start(bf16[4,48,768]{2,1,0:T(8,128)(2,1)} %bitcast.5), calls=%async_computation.2 | async-start | bytes 589824 | tf_op jit(solution)/shard_map/all_to_all | solution.py:133
  71.3 0.1 convert_reduce_fusion
  71.4 7.9 %collective-permute-start.3 = (bf16[112,768]{1,0:T(8,128)(2,1)S(1)}, bf16[112,768]{1,0:T(8,128)(2,1)S(1)}, u32[]{:S(2)}, u32[]{:S(2)}) collective-permute-start(bf16[112,768]{1,0:T(8,128)(2,1)S(1)} %convert_element_type.71), channel_id=1, source_target_pairs={{0,256},{256,0},{1,257},{257,1},{2,258},{258,2},{3,259},{259,3},{4... | collective-permute-start | bytes 516104 | tf_op jit(solution)/shard_map/ppermute | solution.py:96
  79.3 0.0 all-to-all-done.2
  79.3 1.0 convert_reduce_fusion.1
  80.3 12.5 %all_gather.21 = bf16[2,48,768]{2,1,0:T(8,128)(2,1)S(1)} all-gather(bf16[1,48,768]{2,1,0:T(8,128)(2,1)S(1)} %bitcast_convert_fusion), channel_id=1, replica_groups=mesh['za'=2,'zb'=2,'zc'=2,'zhi'=2,'x'=4,'core'=2,'y'=4] {'za'}, dimensions={0}, use_global_device_ids=true | all-gather | bytes 221184 | tf_op jit(solution)/shard_map/all_gather | solution.py:155
  92.9 0.0 collective-permute-done.3
  93.0 11.4 %all_gather.22 = bf16[2,160,768]{2,1,0:T(8,128)(2,1)S(1)} all-gather(bf16[1,160,768]{2,1,0:T(8,128)(2,1)S(1)} %fusion.14), channel_id=1, replica_groups=mesh['za'=2,'zb'=2,'zc'=2,'zhi'=2,'x'=4,'core'=2,'y'=4] {'core'}, dimensions={0}, use_global_device_ids=true | all-gather | bytes 737280 | tf_op jit(solution)/shard_map/all_gather | solution.py:140
  104.3 0.5 fusion.5
  104.9 19.5 %all_gather.23.g = bf16[640,768]{1,0:T(8,128)(2,1)S(1)} all-gather(bf16[160,768]{1,0:T(8,128)(2,1)S(1)} %fusion.5), channel_id=1, replica_groups=mesh['za'=2,'zb'=2,'zc'=2,'zhi'=2,'x'=4,'core'=2,'y'=4] {'zb','zc'}, dimensions={0}, use_global_device_ids=true | all-gather | bytes 1228800 | tf_op jit(solution)/shard_map/all_gather | solution.py:158
  124.4 0.0 copy-done.3
  124.4 1.2 shard_map.77
  125.6 1.0 copy-done.8
  126.5 5.1 %all-to-all-start.3 = ((bf16[16,40,768]{2,1,0:T(8,128)(2,1)}), bf16[16,40,768]{2,1,0:T(8,128)(2,1)}, u32[]{:S(2)}, u32[]{:S(2)}) async-start(bf16[16,40,768]{2,1,0:T(8,128)(2,1)} %bitcast.37), calls=%async_computation.3 | async-start | bytes 1966080 | tf_op jit(solution)/shard_map/all_to_all | solution.py:161
  131.6 0.0 copy-start.10
  131.7 0.8 slice_select_fusion
  132.5 3.7 %collective-permute-start.4 = (bf16[640,384]{1,0:T(8,128)(2,1)}, bf16[640,384]{1,0:T(8,128)(2,1)}, u32[]{:S(2)}, u32[]{:S(2)}) collective-permute-start(bf16[640,384]{1,0:T(8,128)(2,1)} %slice_select_fusion), channel_id=1, source_target_pairs={{0,4},{4,0},{1,5},{5,1},{2,6},{6,2},{3,7},{7,3},{8,12},{12,8},{9,1... | collective-permute-start | bytes 1474568 | tf_op jit(solution)/shard_map/ppermute | solution.py:96
  136.2 1.8 %collective-permute-done.4.k = bf16[640,384]{1,0:T(8,128)(2,1)} collective-permute-done((bf16[640,384]{1,0:T(8,128)(2,1)}, bf16[640,384]{1,0:T(8,128)(2,1)}, u32[]{:S(2)}, u32[]{:S(2)}) %collective-permute-start.4) | collective-permute-done | bytes 491552 | tf_op jit(solution)/shard_map/ppermute | solution.py:96
  138.0 3.7 %shard_map.78 = (f32[768,384]{1,0:T(8,128)}, f32[384,768]{1,0:T(8,128)}) custom-call(s32[1]{0:T(128)} %bitcast.place.core, bf16[640,768]{1,0:T(8,128)(2,1)S(1)} %bitcast.36, bf16[640,768]{1,0:T(8,128)(2,1)S(1)} %copy-done.10, bf16[640,768]{1,0:T(8,128)(2,1)S(1)} %all_gather.23.g, bf16[640,384]{1,0:T(8,128)(2,1)} %collective-permute-done.4.k), custom_call_target="tpu_custom_call" | custom-call | flops 754974720 | bytes 5000000 | tf_op jit(solution)/shard_map/pallas_call | solution.py:84
  141.7 4.4 %all-to-all-done.3 = bf16[16,40,768]{2,1,0:T(8,128)(2,1)} async-done(((bf16[16,40,768]{2,1,0:T(8,128)(2,1)}), bf16[16,40,768]{2,1,0:T(8,128)(2,1)}, u32[]{:S(2)}, u32[]{:S(2)}) %all-to-all-start.3) | async-done | bytes 983072 | tf_op jit(solution)/shard_map/all_to_all | solution.py:161
  146.1 1.4 reduce_sum.35
  147.4 18.2 %all-gather = bf16[160,768]{1,0:T(8,128)(2,1)S(1)} all-gather(bf16[40,768]{1,0:T(8,128)(2,1)S(1)} %reduce_sum.35), channel_id=2, replica_groups=mesh['za'=2,'zb'=2,'zc'=2,'zhi'=2,'x'=4,'core'=2,'y'=4] {'zhi','core'}, dimensions={0}, use_global_device_ids=true | all-gather | bytes 307200 | tf_op jit(solution)/shard_map/all_gather | solution.py:166
  165.6 0.1 reshape.110
  165.8 0.0 copy-done.11
  165.8 0.0 copy-done.12
  165.8 0.6 fusion.17
  (23 shorter events, 0.2 us)
Async XLA Ops:
  23.5 5.2 %copy-start = (bf16[768,384]{1,0:T(8,128)(2,1)S(1)}, bf16[768,384]{1,0:T(8,128)(2,1)}, u32[]{:S(2)}) copy-start(bf16[768,384]{1,0:T(8,128)(2,1)} %own_in.5) | copy-start | bytes 1769476
  23.5 7.6 %copy-start.1 = (bf16[384,768]{1,0:T(8,128)(2,1)S(1)}, bf16[384,768]{1,0:T(8,128)(2,1)}, u32[]{:S(2)}) copy-start(bf16[384,768]{1,0:T(8,128)(2,1)} %own_out.5) | copy-start | bytes 1769476
  23.5 20.4 %all-to-all-start = ((bf16[16,40,768]{2,1,0:T(8,128)(2,1)}), bf16[16,40,768]{2,1,0:T(8,128)(2,1)S(1)}, u32[]{:S(2)}, u32[]{:S(2)}) async-start(bf16[16,40,768]{2,1,0:T(8,128)(2,1)} %broadcast_in_dim.2), calls=%async_computation | async-start | bytes 1966080 | tf_op jit(solution)/shard_map/all_to_all | solution.py:117
  28.7 4.4 %collective-permute-start = (bf16[768,384]{1,0:T(8,128)(2,1)S(1)}, bf16[768,384]{1,0:T(8,128)(2,1)S(1)}, u32[]{:S(2)}, u32[]{:S(2)}) collective-permute-start(bf16[768,384]{1,0:T(8,128)(2,1)S(1)} %copy-done), channel_id=1, source_target_pairs={{0,4},{4,0},{1,5},{5,1},{2,6},{6,2},{3,7},{7,3},{8,12},{12,8},{9,1... | collective-permute-start | bytes 1769480 | tf_op jit(solution)/shard_map/ppermute | solution.py:96
  31.1 3.9 %collective-permute-start.1 = (bf16[384,768]{1,0:T(8,128)(2,1)S(1)}, bf16[384,768]{1,0:T(8,128)(2,1)S(1)}, u32[]{:S(2)}, u32[]{:S(2)}) collective-permute-start(bf16[384,768]{1,0:T(8,128)(2,1)S(1)} %copy-done.1), channel_id=1, source_target_pairs={{0,4},{4,0},{1,5},{5,1},{2,6},{6,2},{3,7},{7,3},{8,12},{12,8},{9,1... | collective-permute-start | bytes 1769480 | tf_op jit(solution)/shard_map/ppermute | solution.py:96
  33.1 22.0 %copy-start.2 = (bf16[768,384]{1,0:T(8,128)(2,1)}, bf16[768,384]{1,0:T(8,128)(2,1)S(1)}, u32[]{:S(2)}) copy-start(bf16[768,384]{1,0:T(8,128)(2,1)S(1)} %collective-permute-done.got_in) | copy-start | bytes 1769476
  35.0 0.8 copy-start.4
  44.0 1.1 copy-start.5
  46.8 20.4 %all-to-all-start.1 = ((bf16[4,112,768]{2,1,0:T(8,128)(2,1)}), bf16[4,112,768]{2,1,0:T(8,128)(2,1)S(1)}, u32[]{:S(2)}, u32[]{:S(2)}) async-start(bf16[4,112,768]{2,1,0:T(8,128)(2,1)} %bitcast.3), calls=%async_computation.1 | async-start | bytes 1376256 | tf_op jit(solution)/shard_map/all_to_all | solution.py:133
  50.3 7.2 %collective-permute-start.2 = (bf16[640,768]{1,0:T(8,128)(2,1)S(1)}, bf16[640,768]{1,0:T(8,128)(2,1)S(1)}, u32[]{:S(2)}, u32[]{:S(2)}) collective-permute-start(bf16[640,768]{1,0:T(8,128)(2,1)S(1)} %bitcast.34), channel_id=1, source_target_pairs={{0,4},{4,0},{1,5},{5,1},{2,6},{6,2},{3,7},{7,3},{8,12},{12,8},{9,1... | collective-permute-start | bytes 2949128 | tf_op jit(solution)/shard_map/ppermute | solution.py:96
  55.1 1.1 copy-start.6
  57.5 0.9 copy-start.9
  67.2 12.1 %all-to-all-start.2 = ((bf16[4,48,768]{2,1,0:T(8,128)(2,1)}), bf16[4,48,768]{2,1,0:T(8,128)(2,1)}, u32[]{:S(2)}, u32[]{:S(2)}) async-start(bf16[4,48,768]{2,1,0:T(8,128)(2,1)} %bitcast.5), calls=%async_computation.2 | async-start | bytes 589824 | tf_op jit(solution)/shard_map/all_to_all | solution.py:133
  71.4 21.5 %collective-permute-start.3 = (bf16[112,768]{1,0:T(8,128)(2,1)S(1)}, bf16[112,768]{1,0:T(8,128)(2,1)S(1)}, u32[]{:S(2)}, u32[]{:S(2)}) collective-permute-start(bf16[112,768]{1,0:T(8,128)(2,1)S(1)} %convert_element_type.71), channel_id=1, source_target_pairs={{0,256},{256,0},{1,257},{257,1},{2,258},{258,2},{3,259},{259,3},{4... | collective-permute-start | bytes 516104 | tf_op jit(solution)/shard_map/ppermute | solution.py:96
  104.3 20.0 %copy-start.3 = (bf16[768,384]{1,0:T(8,128)(2,1)S(1)}, bf16[768,384]{1,0:T(8,128)(2,1)}, u32[]{:S(2)}) copy-start(bf16[768,384]{1,0:T(8,128)(2,1)} %copy-done.2) | copy-start | bytes 1769476
  104.3 20.0 %copy-start.7 = (bf16[384,768]{1,0:T(8,128)(2,1)S(1)}, bf16[384,768]{1,0:T(8,128)(2,1)}, u32[]{:S(2)}) copy-start(bf16[384,768]{1,0:T(8,128)(2,1)} %copy-done.4) | copy-start | bytes 1769476
  125.6 1.0 copy-start.8
  126.5 19.5 %all-to-all-start.3 = ((bf16[16,40,768]{2,1,0:T(8,128)(2,1)}), bf16[16,40,768]{2,1,0:T(8,128)(2,1)}, u32[]{:S(2)}, u32[]{:S(2)}) async-start(bf16[16,40,768]{2,1,0:T(8,128)(2,1)} %bitcast.37), calls=%async_computation.3 | async-start | bytes 1966080 | tf_op jit(solution)/shard_map/all_to_all | solution.py:161
  131.6 6.4 %copy-start.10 = (bf16[640,768]{1,0:T(8,128)(2,1)S(1)}, bf16[640,768]{1,0:T(8,128)(2,1)}, u32[]{:S(2)}) copy-start(bf16[640,768]{1,0:T(8,128)(2,1)} %copy-done.9) | copy-start | bytes 2949124
  132.5 5.5 %collective-permute-start.4 = (bf16[640,384]{1,0:T(8,128)(2,1)}, bf16[640,384]{1,0:T(8,128)(2,1)}, u32[]{:S(2)}, u32[]{:S(2)}) collective-permute-start(bf16[640,384]{1,0:T(8,128)(2,1)} %slice_select_fusion), channel_id=1, source_target_pairs={{0,4},{4,0},{1,5},{5,1},{2,6},{6,2},{3,7},{7,3},{8,12},{12,8},{9,1... | collective-permute-start | bytes 1474568 | tf_op jit(solution)/shard_map/ppermute | solution.py:96
  146.1 19.7 %copy-start.11 = (bf16[10,768]{1,0:T(8,128)(2,1)S(1)}, bf16[10,768]{1,0:T(8,128)(2,1)}, u32[]{:S(2)}) copy-start(bf16[10,768]{1,0:T(8,128)(2,1)} %param.7) | copy-start | bytes 46084
  146.1 19.7 %copy-start.12 = (bf16[10,768]{1,0:T(8,128)(2,1)S(1)}, bf16[10,768]{1,0:T(8,128)(2,1)}, u32[]{:S(2)}) copy-start(bf16[10,768]{1,0:T(8,128)(2,1)} %param.4) | copy-start | bytes 46084
